TPU v7x, 256 devices: a whole 4x4x8 slice. The times are simulated.
256 devices in a mesh: phase: 32 (over z_lo, y, x), lat: 8 (over z_hi, core).
Axes of the slice: x: 4, y: 4, z: 8 (z_hi: 4, z_lo: 2; z = z_hi * 2 + z_lo), core: 2. Of those that a mesh axis runs over, the one named last changes fastest.
Arguments:
- state_now: float32 [3, 256, 1024], P(None, ('lat', 'phase')), may hold values from -4 to 4
- ocean_depth: float32 [256, 1024], P('lat'), may hold values from 0.5 to 1.5
- coriolis: float32 [256], P('lat'), may hold values from -0.4 to 0.4
- phase_times: float32 [32], P('phase'), may hold values from -6 to 6
- phase_weights: float32 [32], P('phase'), may hold values from 0.003125 to 0.125
Outputs:
- state_next: float32 [3, 256, 1024], P(None, ('lat', 'phase'))
- tendency: float32 [3, 256, 1024], P(None, ('lat', 'phase'))
All inputs are finite; a program needn't handle non-finite values.
Results may differ from a plain program's by a relative error of at most 0.00002.
Values sent between devices are 32-bit elements; how exact they have to be, the bound alone decides.
No kernel may reach another device: no remote copies, remote signals or barrier semaphores. Data moves between devices by JAX's collectives and lax.ppermute only.
A program may use at most 64 MiB of HBM per device.

v0:
```python
import math

import jax
import jax.numpy as jnp
from jax import lax
from jax.sharding import PartitionSpec as P

DEG = 8
DEPTH = 4


radius_scale = 2.5
time_step = 0.5
series_terms = 20


def extended_2(shard, sides, width):
    for axis, dim in sides:
        devices, length = (lax.axis_size(axis), shard.shape[dim])
        up = [(i, (i + 1) % devices) for i in range(devices - 1)]
        down = [(j, i) for i, j in up]
        last = lax.slice_in_dim(shard, length - width, length, axis=dim)
        first = lax.slice_in_dim(shard, 0, width, axis=dim)
        before = lax.ppermute(last, axis, up)
        after = lax.ppermute(first, axis, down)
        shard = jnp.concatenate([before, shard, after], axis=dim)
    return shard


def along_lon(values):
    return (jnp.roll(values, -1, axis=-1) - jnp.roll(values, 1, axis=-1)) * 0.5


def along_lat(values):
    return (values[..., 2:, :] - values[..., :-2, :]) * 0.5


def interior(values):
    return values[..., 1:-1, :]


def wave_operator(fields, coefficients):
    height = fields[:, 0]
    eastward = fields[:, 1]
    northward = fields[:, 2]
    depth_field = coefficients[0]
    rotation = coefficients[1]
    out_height = -(along_lon(interior(depth_field * eastward)) + along_lat(depth_field * northward))
    out_east = -along_lon(interior(height)) + interior(rotation * northward)
    out_north = -along_lat(height) - interior(rotation * eastward)
    return jnp.stack([out_height, out_east, out_north], axis=1) / radius_scale


def advection(fields):
    height = fields[:, 0]
    eastward = fields[:, 1]
    northward = fields[:, 2]
    mid_east = interior(eastward)
    mid_north = interior(northward)
    out_height = -(along_lon(interior(height * eastward)) + along_lat(height * northward))
    out_east = -(mid_east * along_lon(mid_east) + mid_north * along_lat(eastward))
    out_north = -(mid_east * along_lon(mid_north) + mid_north * along_lat(northward))
    return jnp.stack([out_height, out_east, out_north], axis=1)


def series_coeffs(sample_time):
    half_time = sample_time * 0.5
    square = half_time * half_time
    result = []
    for degree in range(DEG + 1):
        summed = jnp.zeros_like(sample_time)
        term_sq = jnp.ones_like(sample_time)
        for series in range(series_terms):
            factor = (-1.0) ** series / (math.factorial(series) * math.factorial(series + degree))
            summed = summed + factor * term_sq
            term_sq = term_sq * square
        result.append(summed * half_time**degree)
    return result


def per_device(state_now, ocean_depth, coriolis, phase_times, phase_weights):
    tile_rows = ocean_depth.shape[0]
    stacked = jnp.stack([ocean_depth, jnp.broadcast_to(coriolis[:, None], ocean_depth.shape)])
    coefficients = extended_2(stacked, (("lat", 1),), DEPTH)
    forward = series_coeffs(phase_times)
    backward = series_coeffs(-phase_times)

    def band_coeffs(margin):
        return coefficients[:, DEPTH - margin : DEPTH + tile_rows + margin]

    def exponential(fields, series):
        accumulated = series[0][:, None, None, None] * fields
        previous = None
        current = fields
        for degree in range(1, DEG + 1):
            extended = extended_2(current, (("lat", 2),), 1)
            applied = wave_operator(extended, band_coeffs(1))
            advanced = applied if previous is None else 2.0 * applied + previous
            accumulated = accumulated + 2.0 * series[degree][:, None, None, None] * advanced
            previous = current
            current = advanced
        return accumulated

    def averaged(whole_tile):
        samples = whole_tile[None]
        waves = exponential(samples, forward)
        rimmed = extended_2(waves, (("lat", 2),), 1)
        pulled = advection(rimmed)
        returned = exponential(pulled, backward)
        return jnp.sum(phase_weights[:, None, None, None] * returned, axis=0)

    whole_tile = lax.all_gather(state_now, "phase", axis=1, tiled=True)

    def summed_whole(partial_value):
        return lax.psum(partial_value, "phase")

    first = summed_whole(averaged(whole_tile))
    middle = whole_tile + time_step * first
    second = summed_whole(averaged(middle))
    tendency_tile = 0.5 * (first + second)
    share = state_now.shape[1]
    start = lax.axis_index("phase") * share
    tendency = lax.dynamic_slice_in_dim(tendency_tile, start, share, 1)
    state_next = state_now + time_step * tendency
    return (state_next, tendency)


def solution(mesh):
    placed = (P(None, ("lat", "phase"), None), P("lat", None), P("lat"), P("phase"), P("phase"))
    return jax.shard_map(
        per_device,
        mesh=mesh,
        in_specs=placed,
        out_specs=(P(None, ("lat", "phase"), None), P(None, ("lat", "phase"), None)),
        check_vma=False,
    )
```

profile of v0, /device:TPU:64, one launch (start us, length us, event | category | flops | bytes accessed | tf_op | source)
XLA Modules:
  0.0 1049.4 jit_solution(13986377715848703288)
XLA Ops:
  7.9 84.6 %all_gather.3 = f32[3,32,1024]{2,0,1:T(4,128)S(1)} all-gather(f32[3,1,1024]{2,0,1:T(4,128)S(1)} %copy.21), channel_id=1, replica_groups=mesh['phase'=32,'lat'=8] {'phase'}, dimensions={1}, use_global_device_ids=true | all-gather | bytes 405504 | tf_op jit(solution)/shard_map/all_gather | solution.py:112
  109.4 6.6 collective-permute-start.4
  130.4 5.8 collective-permute-start.8
  140.6 5.8 collective-permute-start.10
  150.5 5.8 collective-permute-start.12
  160.7 5.8 collective-permute-start.14
  170.8 5.8 collective-permute-start.16
  181.2 5.8 collective-permute-start.18
  201.3 5.8 collective-permute-start.22
  211.2 5.8 collective-permute-start.24
  221.1 5.8 collective-permute-start.26
  241.1 5.8 collective-permute-start.30
  251.1 5.8 collective-permute-start.32
  261.1 5.8 collective-permute-start.34
  272.2 296.7 %all-reduce.3.cloned.1.call-done = f32[3,32,1024]{2,1,0:T(8,128)} async-done(((f32[3,32,1024]{2,1,0:T(8,128)}), f32[3,32,1024]{2,1,0:T(8,128)}) %all-reduce.3.cloned.1.call-update) | async-done | bytes 393232 | tf_op jit(solution)/shard_map/psum | solution.py:115
  579.3 6.5 collective-permute-start.38
  590.0 5.8 collective-permute-start.40
  599.9 5.8 collective-permute-start.42
  609.9 5.8 collective-permute-start.44
  619.8 5.8 collective-permute-start.46
  629.8 5.8 collective-permute-start.48
  639.9 5.8 collective-permute-start.50
  650.2 5.8 collective-permute-start.52
  741.1 299.9 %all-reduce.5.cloned.1.call-done = f32[3,32,1024]{2,1,0:T(8,128)} async-done(((f32[3,32,1024]{2,1,0:T(8,128)}), f32[3,32,1024]{2,1,0:T(8,128)}) %all-reduce.5.cloned.1.call-update) | async-done | bytes 393232 | tf_op jit(solution)/shard_map/psum | solution.py:115
  (513 shorter events, 227.2 us)
Async XLA Ops:
  7.2 561.7 %all-reduce.3.cloned.1.call-start = ((), (), s32[]{:S(2)}) async-start(), calls=%async_computation | async-start | bytes 786432 | tf_op jit(solution)/shard_map/psum | solution.py:115
  92.8 13.2 %collective-permute-start.2 = (f32[1,3,1,1024]{3,2,1,0:T(1,128)S(1)}, f32[1,3,1,1024]{3,2,1,0:T(1,128)S(1)}, u32[]{:S(2)}, u32[]{:S(2)}) collective-permute-start(f32[1,3,1,1024]{3,2,1,0:T(1,128)S(1)} %get-tuple-element.240), channel_id=1, source_target_pairs={{0,1},{1,2},{2,3},{3,4},{4,5},{5,6},{6,7},{8,9},{9,10},{10,11},{11... | collective-permute-start | bytes 36872 | tf_op jit(solution)/shard_map/ppermute | solution.py:24
  94.8 11.2 %collective-permute-start.3 = (f32[1,3,1,1024]{3,2,1,0:T(1,128)S(1)}, f32[1,3,1,1024]{3,2,1,0:T(1,128)S(1)}, u32[]{:S(2)}, u32[]{:S(2)}) collective-permute-start(f32[1,3,1,1024]{3,2,1,0:T(1,128)S(1)} %get-tuple-element.241), channel_id=1, source_target_pairs={{1,0},{2,1},{3,2},{4,3},{5,4},{6,5},{7,6},{9,8},{10,9},{11,10},{12... | collective-permute-start | bytes 36872 | tf_op jit(solution)/shard_map/ppermute | solution.py:25
  109.4 8.6 collective-permute-start.4
  130.4 7.7 collective-permute-start.8
  140.6 7.7 collective-permute-start.10
  150.5 8.4 collective-permute-start.12
  160.7 7.9 collective-permute-start.14
  170.8 7.9 collective-permute-start.16
  181.2 7.7 collective-permute-start.18
  191.4 7.7 collective-permute-start.20
  201.3 7.7 collective-permute-start.22
  211.2 7.7 collective-permute-start.24
  221.1 7.7 collective-permute-start.26
  231.1 7.9 collective-permute-start.28
  241.1 7.7 collective-permute-start.30
  251.1 7.7 collective-permute-start.32
  261.1 8.4 collective-permute-start.34
  272.2 768.8 %all-reduce.5.cloned.1.call-start = ((), (), s32[]{:S(2)}) async-start(), calls=%async_computation.1 | async-start | bytes 786432 | tf_op jit(solution)/shard_map/psum | solution.py:115
  579.3 8.4 collective-permute-start.38
  590.0 7.7 collective-permute-start.40
  629.8 7.7 collective-permute-start.48
  639.9 7.7 collective-permute-start.50
  670.2 7.9 collective-permute-start.56
  (51 other events, 537.9 us)
Sparse Core Ops, SparseCore 0:
  272.3 296.5 all-reduce.2
  741.2 299.7 all-reduce.4
where the time goes:
time: 1050 us
  waiting for transfers between devices  643 us (61%)
  starting transfers between devices  267 us (25%)
  blocking collectives  84.6 us (8%)
  other arithmetic  21 us (2%)
  between operations  18.7 us (2%)
  local copies, waits for them, and re-layouts  15.1 us (1%)
    psum x2, waiting for transfers between devices, summed_whole(): return lax.psum(partial_value, 'phase')  597 us
    ppermute x35, starting transfers between devices, extended_2(): before = lax.ppermute(last, axis, up)  193 us
    all_gather x1, blocking collectives, per_device(): whole_tile = lax.all_gather(state_now, 'phase', axis=1, tiled=True)  84.6 us
    ppermute x35, starting transfers between devices, extended_2(): after = lax.ppermute(first, axis, down)  74.4 us
    ppermute x35, waiting for transfers between devices, extended_2(): after = lax.ppermute(first, axis, down)  46.3 us
  transfers between devices with their start and end apart: 72, of which 36 were waited for; matrix products, arithmetic and copies ran while one was open for 0% of the time, Pallas kernels for 0%

commit v1 on v0

v1 whole, which is shorter than its diff:
```python
import functools
import math

import jax
import jax.numpy as jnp
import numpy as np
from jax import lax
from jax.experimental import pallas as pl
from jax.experimental.pallas import tpu as pltpu
from jax.sharding import PartitionSpec as P

DEG = 8
TERMS = DEG + 1
SERIES = 20
SCALE = 2.5
STEP = 0.5

TILE = 32
LANES = 128
LEFT = 48
BASE = 36
BLOCKS = 13
PAD = 8
ROWS = PAD + 8 * BLOCKS + PAD
WIDE = 3 * LANES
SAMPLES = 32

f32 = jnp.float32
bf16 = jnp.bfloat16


def series_table():
    table = np.zeros((24, LANES), np.float32)
    for m in range(SERIES):
        for k in range(TERMS):
            table[m, k] = (-1.0) ** m / (math.factorial(m) * math.factorial(m + k))
    return table


def pack_kernel(row_ref, time_ref, weight_ref, cor_ref, state_ref, depth_ref, table_ref, out_ref, line_ref, lines_ref):
    row = row_ref[0]
    lane = lax.broadcasted_iota(jnp.int32, (1, LANES), 1)
    half = time_ref[0] * 0.5
    square = jnp.full((1, LANES), half * half, f32)
    total = jnp.zeros((1, LANES), f32)
    power = jnp.ones((1, LANES), f32)
    for m in range(SERIES):
        total = total + table_ref[m : m + 1, :] * power
        power = power * square
    scale = jnp.ones((1, LANES), f32)
    for k in range(1, TERMS):
        scale = jnp.where((lane >= k) & (lane < TERMS), scale * half, scale)
    forward = total * scale
    forward = jnp.where(lane == 0, forward, 2.0 * forward)
    backward = jnp.where(lane % 2 == 0, forward, -forward) * weight_ref[0]
    cor = jnp.full((1, LANES), cor_ref[row], f32)
    lanes = lax.broadcasted_iota(jnp.int32, (8, LANES), 1)
    mine = lax.broadcasted_iota(jnp.int32, (8, LANES), 0) == lax.rem(row, 8)
    eight = pl.ds(pl.multiple_of(lax.div(row, 8) * 8, 8), 8)
    for q in range(8):
        depth = depth_ref[eight, q * LANES : (q + 1) * LANES]
        line_ref[q : q + 1, :] = jnp.sum(jnp.where(mine, depth, 0.0), axis=0, keepdims=True)
    extras = (forward, backward, None, cor)
    for f in range(4):
        here = state_ref[f] if f < 3 else line_ref[...]
        after = pltpu.roll(here, 7, 0)
        before = pltpu.roll(here, 1, 0)
        for c in range(4):
            start = TILE * c - LEFT
            first, second = (before, here) if start < 0 else (here, after)
            shift = start % LANES
            window = jnp.where(
                lanes < LANES - shift,
                pltpu.roll(first, LANES - shift, 1),
                pltpu.roll(second, LANES - shift, 1),
            )
            if extras[f] is not None:
                window = jnp.where(lanes < TERMS, jnp.broadcast_to(extras[f], (8, LANES)), window)
            lines_ref[f, pl.ds(c, 8, stride=4), :] = window
        out_ref[:, f * LANES : (f + 1) * LANES] = lines_ref[f]


def unpack_kernel(in_ref, state_ref, next_ref, tendency_ref):
    lanes = lax.broadcasted_iota(jnp.int32, (8, LANES), 1)
    for f in range(3):
        line = jnp.zeros((8, LANES), f32)
        for c in range(4):
            piece = in_ref[pl.ds(c, 8, stride=4), :]
            shift = (TILE * (c - f)) % LANES
            if shift:
                piece = pltpu.roll(piece, shift, 1)
            line = jnp.where((lanes >= TILE * c) & (lanes < TILE * (c + 1)), piece, line)
        tendency_ref[f] = line
        next_ref[f] = state_ref[f] + STEP * line


def split(value):
    high = value.astype(bf16)
    return high, (value - high.astype(f32)).astype(bf16)


def tile_kernel(
    place_ref, own_ref, up_ref, down_ref, far_up_ref, far_down_ref, out_ref,
    p_ref, z_ref, w_ref, yh_ref, yl_ref, t_ref, depth_ref, cor_ref, mask_ref, forward_ref, backh_ref, backl_ref,
):
    lat = place_ref[0]

    def rows(block, offset=0, count=1):
        start = PAD + 8 * block + offset
        return slice(start, start + 8 * count)

    for k in range(TERMS + 1):
        p_ref[k, 0 : PAD + 8, :] = jnp.zeros((PAD + 8, WIDE), f32)
        p_ref[k, ROWS - PAD - 8 : ROWS, :] = jnp.zeros((PAD + 8, WIDE), f32)
    p_ref[TERMS] = jnp.zeros((ROWS, WIDE), f32)
    for k in range(TERMS):
        for block in (0, BLOCKS - 1):
            z_ref[k, rows(block), :] = jnp.zeros((8, WIDE), f32)
    for s in range(SAMPLES):
        for block in (0, BLOCKS - 1):
            w_ref[s, rows(block), :] = jnp.zeros((8, WIDE), f32)
    for ref in (depth_ref, cor_ref):
        ref[0 : PAD + 8, :] = jnp.zeros((PAD + 8, LANES), f32)
        ref[ROWS - PAD - 8 : ROWS, :] = jnp.zeros((PAD + 8, LANES), f32)

    def place(ref, start, count, at):
        at = PAD + BASE + at
        piece = ref[start : start + count, :]
        p_ref[0, at : at + count, :] = piece[:, :WIDE]
        depth_ref[at : at + count, :] = piece[:, WIDE:] * 0.4
        cor_ref[at : at + count, :] = jnp.broadcast_to(piece[:, WIDE : WIDE + 1] * 0.8, (count, LANES))

    place(own_ref, 0, TILE, 0)
    place(up_ref, 0, TILE, -TILE)
    place(down_ref, 0, TILE, TILE)
    place(far_up_ref, 6, 2, -TILE - 2)
    place(far_down_ref, 0, 2, 2 * TILE)

    at_row = lax.broadcasted_iota(jnp.int32, (ROWS, LANES), 0) + (TILE * lat - BASE - PAD)
    mask_ref[...] = jnp.where((at_row >= 0) & (at_row < 8 * TILE), 1.0, 0.0).astype(f32)

    term = lax.broadcasted_iota(jnp.int32, (LANES, 256), 0)
    column = lax.broadcasted_iota(jnp.int32, (LANES, 256), 1)
    group = column // 8
    high_at = (group == term) | (group - 10 == term)
    low_at = group - 20 == term
    pick_high = jnp.where(high_at & (term < TERMS), 1.0, 0.0).astype(bf16)
    pick_low = jnp.where(low_at & (term < TERMS), 1.0, 0.0).astype(bf16)
    same = lax.broadcasted_iota(jnp.int32, (256, 256), 0) % 8 == lax.broadcasted_iota(jnp.int32, (256, 256), 1) % 8

    def spread(block):
        value = own_ref[:, block * LANES : (block + 1) * LANES]
        return split(jnp.broadcast_to(value[:, None, :], (SAMPLES, 8, LANES)).reshape(256, LANES))

    def picked(value, pick):
        return jnp.dot(value, pick, preferred_element_type=f32)

    high, low = spread(0)
    forward = picked(high, pick_high) + picked(low, pick_low)
    forward_ref[...] = jnp.where(same, forward, 0.0).astype(bf16)
    high, low = spread(1)
    pick = jnp.where((group == term) & (term < TERMS), 1.0, 0.0).astype(bf16)[:, :LANES]
    back_high = jnp.where(same[:, :LANES], picked(high, pick), 0.0).T
    back_low = jnp.where(same[:, :LANES], picked(low, pick), 0.0).T
    backh_ref[0:80, :] = back_high[0:80].astype(bf16)
    backh_ref[80:160, :] = back_low[0:80].astype(bf16)
    backl_ref[...] = back_high[0:80].astype(bf16)

    def east(value):
        return pltpu.roll(value, LANES - 1, 1) - pltpu.roll(value, 1, 1)

    def operator(ref, k, block):
        mid, up, down = rows(block), rows(block, 1), rows(block, -1)
        h_at, u_at, v_at = slice(0, LANES), slice(LANES, 2 * LANES), slice(2 * LANES, WIDE)
        h, u, v = ref[k, mid, h_at], ref[k, mid, u_at], ref[k, mid, v_at]
        mask, cor = mask_ref[mid, :], cor_ref[mid, :]
        flux = east(depth_ref[mid, :] * u) + (depth_ref[up, :] * ref[k, up, v_at] - depth_ref[down, :] * ref[k, down, v_at])
        out_h = -(mask * flux)
        out_u = cor * v - 0.4 * east(h)
        out_v = mask * (-0.4 * (ref[k, up, h_at] - ref[k, down, h_at])) - cor * u
        return out_h, out_u, out_v

    def fields(ref, k, block):
        return [ref[k, rows(block), f * LANES : (f + 1) * LANES] for f in range(3)]

    def store(ref, k, block, values):
        for f in range(3):
            ref[k, rows(block), f * LANES : (f + 1) * LANES] = values[f]

    def averaged(outer, inner):
        for k in range(1, TERMS):
            for block in range(*outer):
                new = operator(p_ref, k - 1, block)
                if k == 1:
                    new = [0.5 * value for value in new]
                else:
                    new = [a + b for a, b in zip(new, fields(p_ref, k - 2, block))]
                store(p_ref, k, block, new)

        first, last = inner
        for block in range(first, last):
            value = p_ref[:, rows(block), :].reshape(80, WIDE)
            high, low = split(value)
            stacked = jnp.concatenate([high, low, high, jnp.zeros((16, WIDE), bf16)], axis=0)
            waves = jnp.dot(forward_ref[...], stacked, preferred_element_type=f32)
            w_ref[:, rows(block), :] = waves.reshape(SAMPLES, 8, WIDE)

        def advect(s, block):
            mid, up, down = rows(block), rows(block, 1), rows(block, -1)
            h_at, u_at, v_at = slice(0, LANES), slice(LANES, 2 * LANES), slice(2 * LANES, WIDE)
            h, u, v = w_ref[s, mid, h_at], w_ref[s, mid, u_at], w_ref[s, mid, v_at]
            v_up, v_down = w_ref[s, up, v_at], w_ref[s, down, v_at]
            out_h = east(h * u) + (w_ref[s, up, h_at] * v_up - w_ref[s, down, h_at] * v_down)
            out_u = u * east(u) + v * (w_ref[s, up, u_at] - w_ref[s, down, u_at])
            out_v = u * east(v) + v * (v_up - v_down)
            return out_h, out_u, out_v

        def pair(n, carry):
            for block in range(first, last):
                one, two = advect(2 * n, block), advect(2 * n + 1, block)
                for f in range(3):
                    high, low = split(jnp.concatenate([one[f], two[f]], axis=0))
                    yh_ref[block, n, :, f * LANES : (f + 1) * LANES] = high
                    yl_ref[block, n, :, f * LANES : (f + 1) * LANES] = low
            return carry

        lax.fori_loop(0, SAMPLES // 2, pair, 0)

        for block in range(first, last):
            high = yh_ref[block].reshape(256, WIDE)
            low = yl_ref[block].reshape(256, WIDE)
            both = jnp.dot(backh_ref[...], high, preferred_element_type=f32)
            total = both[0:80] + both[80:160] + jnp.dot(backl_ref[...], low, preferred_element_type=f32)
            total = total * -0.5
            for k in range(TERMS):
                term_at = total[8 * k : 8 * k + 8]
                z_ref[k, rows(block), 0:LANES] = term_at[:, 0:LANES] * mask_ref[rows(block), :]
                z_ref[k, rows(block), LANES:WIDE] = term_at[:, LANES:WIDE]

        for k in range(DEG - 1, -1, -1):
            for block in range(first, last):
                new = operator(z_ref, k + 1, block)
                if k == 0:
                    new = [0.5 * value for value in new]
                new = [a + b for a, b in zip(new, fields(z_ref, k, block))]
                if k + 2 < TERMS:
                    new = [a + b for a, b in zip(new, fields(z_ref, k + 2, block))]
                store(z_ref, k, block, new)

    averaged((0, 13), (1, 12))
    for block in range(2, 11):
        at = rows(block)
        t_ref[at, :] = z_ref[0, at, :]
        p_ref[0, at, :] = p_ref[0, at, :] + STEP * z_ref[0, at, :]
    averaged((2, 11), (3, 10))
    at = slice(PAD + BASE, PAD + BASE + TILE)
    tendency = 0.5 * (t_ref[at, :] + z_ref[0, at, :])
    lanes = lax.broadcasted_iota(jnp.int32, (TILE, LANES), 1)
    parts = [pltpu.roll(tendency[:, f * LANES : (f + 1) * LANES], (TILE * f - LEFT) % LANES, 1) for f in range(3)]
    out_ref[...] = jnp.where(lanes < TILE, parts[0], jnp.where(lanes < 2 * TILE, parts[1], parts[2]))


def vmem():
    return pl.BlockSpec(memory_space=pltpu.VMEM)


def smem():
    return pl.BlockSpec(memory_space=pltpu.SMEM)


def pack(row, times, weights, cor, state, depth):
    return pl.pallas_call(
        pack_kernel,
        out_shape=jax.ShapeDtypeStruct((TILE, 4 * LANES), f32),
        in_specs=[smem(), smem(), smem(), smem(), vmem(), vmem(), vmem()],
        out_specs=vmem(),
        scratch_shapes=[pltpu.VMEM((8, LANES), f32), pltpu.VMEM((4, TILE, LANES), f32)],
        name="pack",
    )(row, times, weights, cor, state, depth, jnp.asarray(series_table()))


def tile(place, own, up, down, far_up, far_down):
    return pl.pallas_call(
        tile_kernel,
        out_shape=jax.ShapeDtypeStruct((TILE, LANES), f32),
        in_specs=[smem()] + [vmem()] * 5,
        out_specs=vmem(),
        scratch_shapes=[
            pltpu.VMEM((TERMS + 1, ROWS, WIDE), f32),
            pltpu.VMEM((TERMS, ROWS, WIDE), f32),
            pltpu.VMEM((SAMPLES, ROWS, WIDE), f32),
            pltpu.VMEM((BLOCKS, SAMPLES // 2, 16, WIDE), bf16),
            pltpu.VMEM((BLOCKS, SAMPLES // 2, 16, WIDE), bf16),
            pltpu.VMEM((ROWS, WIDE), f32),
            pltpu.VMEM((ROWS, LANES), f32),
            pltpu.VMEM((ROWS, LANES), f32),
            pltpu.VMEM((ROWS, LANES), f32),
            pltpu.VMEM((256, 256), bf16),
            pltpu.VMEM((160, 256), bf16),
            pltpu.VMEM((80, 256), bf16),
        ],
        compiler_params=pltpu.CompilerParams(vmem_limit_bytes=48 * 1024 * 1024),
        name="tile",
    )(place, own, up, down, far_up, far_down)


def unpack(columns, state):
    shape = jax.ShapeDtypeStruct((3, 8, LANES), f32)
    return pl.pallas_call(
        unpack_kernel,
        out_shape=(shape, shape),
        in_specs=[vmem(), vmem()],
        out_specs=(vmem(), vmem()),
        name="unpack",
    )(columns, state)


def per_device(tiles, state_now, ocean_depth, coriolis, phase_times, phase_weights):
    state = state_now.reshape(3, 8, LANES)
    row = lax.axis_index("phase").astype(jnp.int32)[None]
    lat = lax.axis_index("lat").astype(jnp.int32)[None]
    message = pack(row, phase_times, phase_weights, coriolis, state, ocean_depth)
    own = lax.all_to_all(message, "phase", 0, 0, tiled=True)
    up = lax.ppermute(own, "lat", [(i, i + 1) for i in range(tiles - 1)])
    down = lax.ppermute(own, "lat", [(i + 1, i) for i in range(tiles - 1)])
    far_up = lax.ppermute(own[TILE - 8 :], "lat", [(i, i + 2) for i in range(tiles - 2)])
    far_down = lax.ppermute(own[:8], "lat", [(i + 2, i) for i in range(tiles - 2)])
    columns = tile(lat, own, up, down, far_up, far_down)
    columns = lax.all_to_all(columns, "phase", 0, 0, tiled=True)
    state_next, tendency = unpack(columns, state)
    return state_next.reshape(state_now.shape), tendency.reshape(state_now.shape)


def solution(mesh):
    rows = P(None, ("lat", "phase"), None)
    return jax.shard_map(
        functools.partial(per_device, mesh.shape["lat"]),
        mesh=mesh,
        in_specs=(rows, P("lat", None), P("lat"), P("phase"), P("phase")),
        out_specs=(rows, rows),
        check_vma=False,
    )
```

time: 1050 us -> 65.2 us (0.06)
  waiting for transfers between devices: 643 us -> 6.17 us
  starting transfers between devices: 267 us -> 11.7 us
  blocking collectives: 84.6 us -> 28.5 us
  other arithmetic: 21 us -> 0 us
  between operations: 18.7 us -> 2 us
  Pallas kernels: 0 us -> 15.4 us
  local copies, waits for them, and re-layouts: 15.1 us -> 0.92 us
    psum x2 -> x0, waiting for transfers between devices: 597 us -> none  [summed_whole(): return lax.psum(partial_value, 'phase')]
    ppermute x70 -> x4, starting transfers between devices: 267 us -> 11.7 us  [the longest x1 5.49 us: per_device(): lax.ppermute(own[TILE - 8:], 'lat', [(i, i + 2) for i in range(tiles - 2)])]
    all_gather x1 -> x0, blocking collectives: 84.6 us -> none  [per_device(): whole_tile = lax.all_gather(state_now, 'phase', axis=1, tiled=True)]
    ppermute x70 -> x4, waiting for transfers between devices: 46.4 us -> 6.17 us  [the longest x1 6.17 us: per_device(): lax.ppermute(own[:8], 'lat', [(i + 2, i) for i in range(tiles - 2)])]
    all_to_all x0 -> x2, blocking collectives: none -> 28.5 us  [the longest x1 16.8 us: per_device(): own = lax.all_to_all(message, 'phase', 0, 0, tiled=True)]
    pallas_call x0 -> x3, Pallas kernels: none -> 15.4 us  [the longest x1 12.3 us: tile(): pl.pallas_call(tile_kernel, out_shape=jax.ShapeDtypeStruct((TILE, LANES),...]
    slice x174 -> x1, local copies, waits for them, and re-layouts: 12.9 us -> 0.01 us  [per_device(): own[:8]]
    add x60 -> x0, other arithmetic: 10.9 us -> none  [the longest x32 3.92 us: wave_operator(): out_east = -along_lon(interior(height)) + interior(rotation * northward)]
  transfers between devices with their start and end apart: 72 -> 4, of which waited for: 36 -> 1; matrix products, arithmetic and copies ran while one was open for 0% -> 0% of each run, Pallas kernels for 0% -> 0%
where the time goes in v1:
time: 65.2 us; the launch traced here: 64.7 us
  blocking collectives  28.5 us (44%)
  Pallas kernels  15.4 us (24%)
  starting transfers between devices  11.7 us (18%)
  waiting for transfers between devices  6.17 us (9%)
  between operations  2 us (3%)
  local copies, waits for them, and re-layouts  0.92 us (1%)
    all_to_all x1, blocking collectives, per_device(): own = lax.all_to_all(message, 'phase', 0, 0, tiled=True)  16.8 us
    pallas_call x1, Pallas kernels, tile(): pl.pallas_call(tile_kernel, out_shape=jax.ShapeDtypeStruct((TILE, LANES),...  12.3 us
    all_to_all x1, blocking collectives, per_device(): columns = lax.all_to_all(columns, 'phase', 0, 0, tiled=True)  11.7 us
    ppermute x1, waiting for transfers between devices, per_device(): lax.ppermute(own[:8], 'lat', [(i + 2, i) for i in range(tiles - 2)])  6.17 us
    ppermute x1, starting transfers between devices, per_device(): lax.ppermute(own[TILE - 8:], 'lat', [(i, i + 2) for i in range(tiles - 2)])  5.49 us
    ppermute x1, starting transfers between devices, per_device(): up = lax.ppermute(own, 'lat', [(i, i + 1) for i in range(tiles - 1)])  2.41 us
    ppermute x1, starting transfers between devices, per_device(): lax.ppermute(own[:8], 'lat', [(i + 2, i) for i in range(tiles - 2)])  1.92 us
    ppermute x1, starting transfers between devices, per_device(): down = lax.ppermute(own, 'lat', [(i + 1, i) for i in range(tiles - 1)])  1.91 us
  transfers between devices with their start and end apart: 4, of which 1 were waited for; matrix products, arithmetic and copies ran while one was open for 0% of the time, Pallas kernels for 0%

profile of v1, /device:TPU:64, one launch (start us, length us, event | category | flops | bytes accessed | tf_op | source)
XLA Modules:
  0.0 64.7 jit_solution(7184115667759109457)
XLA Ops:
  1.9 1.6 %pack.1 = f32[32,512]{1,0:T(8,128)} custom-call(s32[1]{0:T(128)} %bitcast.1.row_ref, f32[1]{0:T(128)S(6)} %copy.27.time_ref, f32[1]{0:T(128)S(6)} %copy.28.weight_ref, f32[32]{0:T(128)} %cor_ref.1, f32[3,8,128]{2,1,0:T(8,128)} %bitcast.25, f32[32,1024]{1,0:T(8,128)} %depth_ref.1, f32[24,128]{1,0:T(8,128)} %constant.11.clone.table_ref), custom_call_target="tpu_custom_call" | custom-call | tf_op jit(solution)/shard_map/pack/pallas_call | solution.py:272
  3.6 0.9 %copy.12 = f32[32,1,512]{2,1,0:T(1,128)S(1)} copy(f32[32,1,512]{2,0,1:T(8,128)} %bitcast.23) | data formatting | bytes 131072 | tf_op jit(solution)/shard_map/all_to_all | solution.py:323
  4.5 16.8 %all_to_all.22 = f32[32,1,512]{2,1,0:T(1,128)S(1)} all-to-all(f32[32,1,512]{2,1,0:T(1,128)S(1)} %copy.12), channel_id=1, replica_groups=mesh['phase'=32,'lat'=8] {'phase'}, dimensions={0} | all-to-all | bytes 131072 | tf_op jit(solution)/shard_map/all_to_all | solution.py:323
  21.3 1.9 %collective-permute-start.1 = (f32[32,512]{1,0:T(8,128)S(1)}, f32[32,512]{1,0:T(8,128)S(1)}, u32[]{:S(2)}, u32[]{:S(2)}) collective-permute-start(f32[32,512]{1,0:T(8,128)S(1)} %bitcast.19), channel_id=1, source_target_pairs={{1,0},{2,1},{3,2},{4,3},{5,4},{6,5},{7,6},{9,8},{10,9},{11,10},{12... | collective-permute-start | bytes 196616 | tf_op jit(solution)/shard_map/ppermute | solution.py:325
  23.2 2.4 %collective-permute-start = (f32[32,512]{1,0:T(8,128)S(1)}, f32[32,512]{1,0:T(8,128)S(1)}, u32[]{:S(2)}, u32[]{:S(2)}) collective-permute-start(f32[32,512]{1,0:T(8,128)S(1)} %bitcast.20), channel_id=1, source_target_pairs={{0,1},{1,2},{2,3},{3,4},{4,5},{5,6},{6,7},{8,9},{9,10},{10,11},{11... | collective-permute-start | bytes 196616 | tf_op jit(solution)/shard_map/ppermute | solution.py:324
  25.7 5.5 %collective-permute-start.2 = (f32[8,512]{1,0:T(8,128)S(1)}, f32[8,512]{1,0:T(8,128)S(1)}, u32[]{:S(2)}, u32[]{:S(2)}) collective-permute-start(f32[8,512]{1,0:T(8,128)S(1)} %bitcast.28), channel_id=1, source_target_pairs={{0,2},{1,3},{2,4},{3,5},{4,6},{5,7},{8,10},{9,11},{10,12},{11,13},... | collective-permute-start | bytes 49160 | tf_op jit(solution)/shard_map/ppermute | solution.py:326
  31.2 1.9 %collective-permute-start.3 = (f32[8,512]{1,0:T(8,128)S(1)}, f32[8,512]{1,0:T(8,128)S(1)}, u32[]{:S(2)}, u32[]{:S(2)}) collective-permute-start(f32[8,512]{1,0:T(8,128)S(1)} %bitcast.27), channel_id=1, source_target_pairs={{2,0},{3,1},{4,2},{5,3},{6,4},{7,5},{10,8},{11,9},{12,10},{13,11},... | collective-permute-start | bytes 49160 | tf_op jit(solution)/shard_map/ppermute | solution.py:327
  33.1 0.0 collective-permute-done.2.far_up_ref
  33.1 6.2 %collective-permute-done.3.far_down_ref = f32[8,512]{1,0:T(8,128)S(1)} collective-permute-done((f32[8,512]{1,0:T(8,128)S(1)}, f32[8,512]{1,0:T(8,128)S(1)}, u32[]{:S(2)}, u32[]{:S(2)}) %collective-permute-start.3) | collective-permute-done | bytes 16416 | tf_op jit(solution)/shard_map/ppermute | solution.py:327
  39.3 0.0 collective-permute-done.1.down_ref
  39.3 0.0 collective-permute-done.up_ref
  39.3 12.3 %tile.1 = f32[32,128]{1,0:T(8,128)S(1)} custom-call(s32[1]{0:T(128)} %bitcast.place_ref, f32[32,512]{1,0:T(8,128)S(1)} %bitcast.21, f32[32,512]{1,0:T(8,128)S(1)} %collective-permute-done.up_ref, f32[32,512]{1,0:T(8,128)S(1)} %collective-permute-done.1.down_ref, f32[8,512]{1,0:T(8,128)S(1)} %collective-permute-done.2.far_up_ref, ...), custom_call_target="tpu_custom_call" | custom-call | tf_op jit(solution)/shard_map/tile/pallas_call | solution.py:283
  51.6 11.7 %all_to_all.23 = f32[32,1,128]{2,1,0:T(1,128)} all-to-all(f32[32,1,128]{2,1,0:T(1,128)S(1)} %bitcast.22), channel_id=1, replica_groups=mesh['phase'=32,'lat'=8] {'phase'}, dimensions={0} | all-to-all | bytes 32768 | tf_op jit(solution)/shard_map/all_to_all | solution.py:329
  63.3 1.4 %unpack.1 = (f32[3,8,128]{2,1,0:T(8,128)}, f32[3,8,128]{2,1,0:T(8,128)}) custom-call(f32[32,128]{1,0:T(8,128)} %bitcast.24, f32[3,8,128]{2,1,0:T(8,128)} %bitcast.26), custom_call_target="tpu_custom_call" | custom-call | tf_op jit(solution)/shard_map/unpack/pallas_call | solution.py:309
  (4 shorter events, 0.0 us)
Async XLA Ops:
  21.3 18.0 %collective-permute-start.1 = (f32[32,512]{1,0:T(8,128)S(1)}, f32[32,512]{1,0:T(8,128)S(1)}, u32[]{:S(2)}, u32[]{:S(2)}) collective-permute-start(f32[32,512]{1,0:T(8,128)S(1)} %bitcast.19), channel_id=1, source_target_pairs={{1,0},{2,1},{3,2},{4,3},{5,4},{6,5},{7,6},{9,8},{10,9},{11,10},{12... | collective-permute-start | bytes 196616 | tf_op jit(solution)/shard_map/ppermute | solution.py:325
  23.2 16.1 %collective-permute-start = (f32[32,512]{1,0:T(8,128)S(1)}, f32[32,512]{1,0:T(8,128)S(1)}, u32[]{:S(2)}, u32[]{:S(2)}) collective-permute-start(f32[32,512]{1,0:T(8,128)S(1)} %bitcast.20), channel_id=1, source_target_pairs={{0,1},{1,2},{2,3},{3,4},{4,5},{5,6},{6,7},{8,9},{9,10},{10,11},{11... | collective-permute-start | bytes 196616 | tf_op jit(solution)/shard_map/ppermute | solution.py:324
  25.7 7.4 %collective-permute-start.2 = (f32[8,512]{1,0:T(8,128)S(1)}, f32[8,512]{1,0:T(8,128)S(1)}, u32[]{:S(2)}, u32[]{:S(2)}) collective-permute-start(f32[8,512]{1,0:T(8,128)S(1)} %bitcast.28), channel_id=1, source_target_pairs={{0,2},{1,3},{2,4},{3,5},{4,6},{5,7},{8,10},{9,11},{10,12},{11,13},... | collective-permute-start | bytes 49160 | tf_op jit(solution)/shard_map/ppermute | solution.py:326
  31.2 8.1 %collective-permute-start.3 = (f32[8,512]{1,0:T(8,128)S(1)}, f32[8,512]{1,0:T(8,128)S(1)}, u32[]{:S(2)}, u32[]{:S(2)}) collective-permute-start(f32[8,512]{1,0:T(8,128)S(1)} %bitcast.27), channel_id=1, source_target_pairs={{2,0},{3,1},{4,2},{5,3},{6,4},{7,5},{10,8},{11,9},{12,10},{13,11},... | collective-permute-start | bytes 49160 | tf_op jit(solution)/shard_map/ppermute | solution.py:327

commit v2 on v1

--- a/solution.py
+++ b/solution.py
@@ -14,6 +14,7 @@
 SERIES = 20
 SCALE = 2.5
 STEP = 0.5
+NLON = 1024
 
 TILE = 32
 LANES = 128
@@ -37,7 +38,7 @@
     return table
 
 
-def pack_kernel(row_ref, time_ref, weight_ref, cor_ref, state_ref, depth_ref, table_ref, out_ref, line_ref, lines_ref):
+def pack_kernel(row_ref, time_ref, weight_ref, cor_ref, state_ref, depth_ref, table_ref, out_ref, line_ref):
     row = row_ref[0]
     lane = lax.broadcasted_iota(jnp.int32, (1, LANES), 1)
     half = time_ref[0] * 0.5
@@ -56,9 +57,8 @@
     cor = jnp.full((1, LANES), cor_ref[row], f32)
     lanes = lax.broadcasted_iota(jnp.int32, (8, LANES), 1)
     mine = lax.broadcasted_iota(jnp.int32, (8, LANES), 0) == lax.rem(row, 8)
-    eight = pl.ds(pl.multiple_of(lax.div(row, 8) * 8, 8), 8)
     for q in range(8):
-        depth = depth_ref[eight, q * LANES : (q + 1) * LANES]
+        depth = depth_ref[:, q * LANES : (q + 1) * LANES]
         line_ref[q : q + 1, :] = jnp.sum(jnp.where(mine, depth, 0.0), axis=0, keepdims=True)
     extras = (forward, backward, None, cor)
     for f in range(4):
@@ -76,8 +76,8 @@
             )
             if extras[f] is not None:
                 window = jnp.where(lanes < TERMS, jnp.broadcast_to(extras[f], (8, LANES)), window)
-            lines_ref[f, pl.ds(c, 8, stride=4), :] = window
-        out_ref[:, f * LANES : (f + 1) * LANES] = lines_ref[f]
+            for core in range(2):
+                out_ref[pl.ds(4 * (TILE * core + c) + f, 8, stride=16), :] = window
 
 
 def unpack_kernel(in_ref, state_ref, next_ref, tendency_ref):
@@ -100,10 +100,11 @@
 
 
 def tile_kernel(
-    place_ref, own_ref, up_ref, down_ref, far_up_ref, far_down_ref, out_ref,
+    place_ref, own_ref, near_ref, far_ref, out_ref,
     p_ref, z_ref, w_ref, yh_ref, yl_ref, t_ref, depth_ref, cor_ref, mask_ref, forward_ref, backh_ref, backl_ref,
 ):
     lat = place_ref[0]
+    core = lax.rem(lat, 2)
 
     def rows(block, offset=0, count=1):
         start = PAD + 8 * block + offset
@@ -123,18 +124,26 @@
         ref[0 : PAD + 8, :] = jnp.zeros((PAD + 8, LANES), f32)
         ref[ROWS - PAD - 8 : ROWS, :] = jnp.zeros((PAD + 8, LANES), f32)
 
-    def place(ref, start, count, at):
+    def place(ref, count, at):
         at = PAD + BASE + at
-        piece = ref[start : start + count, :]
-        p_ref[0, at : at + count, :] = piece[:, :WIDE]
-        depth_ref[at : at + count, :] = piece[:, WIDE:] * 0.4
-        cor_ref[at : at + count, :] = jnp.broadcast_to(piece[:, WIDE : WIDE + 1] * 0.8, (count, LANES))
-
-    place(own_ref, 0, TILE, 0)
-    place(up_ref, 0, TILE, -TILE)
-    place(down_ref, 0, TILE, TILE)
-    place(far_up_ref, 6, 2, -TILE - 2)
-    place(far_down_ref, 0, 2, 2 * TILE)
+        h, u, v, depth, = [ref[pl.ds(f, count, stride=4), :] for f in range(4)]
+        p_ref[0, at : at + count, 0:LANES] = h
+        p_ref[0, at : at + count, LANES : 2 * LANES] = u
+        p_ref[0, at : at + count, 2 * LANES : WIDE] = v
+        depth_ref[at : at + count, :] = depth * 0.4
+        cor_ref[at : at + count, :] = jnp.broadcast_to(depth[:, 0:1] * 0.8, (count, LANES))
+
+    @pl.when(core == 0)
+    def _():
+        place(own_ref, 2 * TILE, 0)
+        place(near_ref, TILE + 2, -TILE - 2)
+        place(far_ref, 2, 2 * TILE)
+
+    @pl.when(core == 1)
+    def _():
+        place(own_ref, 2 * TILE, -TILE)
+        place(near_ref, TILE + 2, TILE)
+        place(far_ref, 2, -TILE - 2)
 
     at_row = lax.broadcasted_iota(jnp.int32, (ROWS, LANES), 0) + (TILE * lat - BASE - PAD)
     mask_ref[...] = jnp.where((at_row >= 0) & (at_row < 8 * TILE), 1.0, 0.0).astype(f32)
@@ -149,7 +158,7 @@
     same = lax.broadcasted_iota(jnp.int32, (256, 256), 0) % 8 == lax.broadcasted_iota(jnp.int32, (256, 256), 1) % 8
 
     def spread(block):
-        value = own_ref[:, block * LANES : (block + 1) * LANES]
+        value = own_ref[pl.ds(block, SAMPLES, stride=4), :]
         return split(jnp.broadcast_to(value[:, None, :], (SAMPLES, 8, LANES)).reshape(256, LANES))
 
     def picked(value, pick):
@@ -269,21 +278,30 @@
 
 
 def pack(row, times, weights, cor, state, depth):
+    grid = pltpu.PrefetchScalarGridSpec(
+        num_scalar_prefetch=1,
+        grid=(1,),
+        in_specs=[
+            smem(), smem(), smem(), vmem(),
+            pl.BlockSpec((8, NLON), lambda i, at: (lax.div(at[0], 8), 0)),
+            vmem(),
+        ],
+        out_specs=vmem(),
+        scratch_shapes=[pltpu.VMEM((8, LANES), f32)],
+    )
     return pl.pallas_call(
         pack_kernel,
-        out_shape=jax.ShapeDtypeStruct((TILE, 4 * LANES), f32),
-        in_specs=[smem(), smem(), smem(), smem(), vmem(), vmem(), vmem()],
-        out_specs=vmem(),
-        scratch_shapes=[pltpu.VMEM((8, LANES), f32), pltpu.VMEM((4, TILE, LANES), f32)],
+        out_shape=jax.ShapeDtypeStruct((2 * TILE * 4, LANES), f32),
+        grid_spec=grid,
         name="pack",
     )(row, times, weights, cor, state, depth, jnp.asarray(series_table()))
 
 
-def tile(place, own, up, down, far_up, far_down):
+def tile(place, own, near, far):
     return pl.pallas_call(
         tile_kernel,
         out_shape=jax.ShapeDtypeStruct((TILE, LANES), f32),
-        in_specs=[smem()] + [vmem()] * 5,
+        in_specs=[smem()] + [vmem()] * 3,
         out_specs=vmem(),
         scratch_shapes=[
             pltpu.VMEM((TERMS + 1, ROWS, WIDE), f32),
@@ -301,7 +319,7 @@
         ],
         compiler_params=pltpu.CompilerParams(vmem_limit_bytes=48 * 1024 * 1024),
         name="tile",
-    )(place, own, up, down, far_up, far_down)
+    )(place, own, near, far)
 
 
 def unpack(columns, state):
@@ -315,28 +333,40 @@
     )(columns, state)
 
 
-def per_device(tiles, state_now, ocean_depth, coriolis, phase_times, phase_weights):
+def per_device(ring, state_now, ocean_depth, coriolis, phase_times, phase_weights):
     state = state_now.reshape(3, 8, LANES)
-    row = lax.axis_index("phase").astype(jnp.int32)[None]
-    lat = lax.axis_index("lat").astype(jnp.int32)[None]
-    message = pack(row, phase_times, phase_weights, coriolis, state, ocean_depth)
-    own = lax.all_to_all(message, "phase", 0, 0, tiled=True)
-    up = lax.ppermute(own, "lat", [(i, i + 1) for i in range(tiles - 1)])
-    down = lax.ppermute(own, "lat", [(i + 1, i) for i in range(tiles - 1)])
-    far_up = lax.ppermute(own[TILE - 8 :], "lat", [(i, i + 2) for i in range(tiles - 2)])
-    far_down = lax.ppermute(own[:8], "lat", [(i + 2, i) for i in range(tiles - 2)])
-    columns = tile(lat, own, up, down, far_up, far_down)
+    row = lax.axis_index("phase").astype(jnp.int32)
+    core = lax.axis_index("core").astype(jnp.int32)
+    lat = 2 * lax.axis_index("ring").astype(jnp.int32) + core
+    message = pack(row[None], phase_times, phase_weights, coriolis, state, ocean_depth)
+    own = lax.all_to_all(message, ("core", "phase"), 0, 0, tiled=True)
+    devices = ("phase", "ring", "core")
+
+    def index(phase, at, of):
+        return (phase * ring + at) * 2 + of
+
+    def pairs(step):
+        moves = [(at, at + step, 0) for at in range(ring)] + [(at, at - step, 1) for at in range(ring)]
+        return [(index(p, a, c), index(p, b, c)) for p in range(TILE) for a, b, c in moves if 0 <= b < ring]
+
+    near = lax.dynamic_slice_in_dim(own, jnp.where(core == 0, 4 * (TILE - 2), 0), 4 * (TILE + 2), 0)
+    far = lax.dynamic_slice_in_dim(own, jnp.where(core == 0, 0, 4 * (2 * TILE - 2)), 8, 0)
+    near = lax.ppermute(near, devices, pairs(1))
+    far = lax.ppermute(far, devices, pairs(-1))
+    columns = tile(lat[None], own, near, far)
     columns = lax.all_to_all(columns, "phase", 0, 0, tiled=True)
     state_next, tendency = unpack(columns, state)
     return state_next.reshape(state_now.shape), tendency.reshape(state_now.shape)
 
 
 def solution(mesh):
-    rows = P(None, ("lat", "phase"), None)
+    phase, lat = mesh.shape["phase"], mesh.shape["lat"]
+    mesh = jax.sharding.Mesh(mesh.devices.reshape(phase, lat // 2, 2), ("phase", "ring", "core"))
+    rows = P(None, ("ring", "core", "phase"), None)
     return jax.shard_map(
-        functools.partial(per_device, mesh.shape["lat"]),
+        functools.partial(per_device, lat // 2),
         mesh=mesh,
-        in_specs=(rows, P("lat", None), P("lat"), P("phase"), P("phase")),
+        in_specs=(rows, P(("ring", "core"), None), P(("ring", "core")), P("phase"), P("phase")),
         out_specs=(rows, rows),
         check_vma=False,
     )

time: 65.2 us -> 60.4 us (0.926)
  blocking collectives: 28.5 us -> 11.8 us
  waiting for transfers between devices: 6.17 us -> 14.2 us
  starting transfers between devices: 11.7 us -> 16.7 us
  local copies, waits for them, and re-layouts: 0.92 us -> 0.02 us
    all_to_all x1 -> x0, blocking collectives: 16.8 us -> none  [per_device(): own = lax.all_to_all(message, 'phase', 0, 0, tiled=True)]
    all_to_all x0 -> x1, starting transfers between devices: none -> 9.29 us  [per_device(): own = lax.all_to_all(message, ('core', 'phase'), 0, 0, tiled=True)]
    all_to_all x0 -> x1, waiting for transfers between devices: none -> 8.5 us  [per_device(): own = lax.all_to_all(message, ('core', 'phase'), 0, 0, tiled=True)]
    ppermute x4 -> x2, starting transfers between devices: 11.7 us -> 7.4 us  [the longest x1 5.48 us: per_device(): near = lax.ppermute(near, devices, pairs(1))]
    all_to_all x1 -> x0, local copies, waits for them, and re-layouts: 0.91 us -> none  [per_device(): own = lax.all_to_all(message, 'phase', 0, 0, tiled=True)]
    ppermute x4 -> x2, waiting for transfers between devices: 6.17 us -> 5.68 us  [the longest x1 5.68 us: per_device(): far = lax.ppermute(far, devices, pairs(-1))]
  transfers between devices with their start and end apart: 4 -> 3, of which waited for: 1 -> 2; matrix products, arithmetic and copies ran while one was open for 0% -> 0% of each run, Pallas kernels for 0% -> 0%
where the time goes in v2:
time: 60.4 us; the launch traced here: 60 us
  starting transfers between devices  16.7 us (28%)
  Pallas kernels  15.3 us (25%)
  waiting for transfers between devices  14.2 us (24%)
  blocking collectives  11.8 us (20%)
  between operations  1.98 us (3%)
    pallas_call x1, Pallas kernels, tile(): pl.pallas_call(tile_kernel, out_shape=jax.ShapeDtypeStruct((TILE, LANES),...  12.3 us
    all_to_all x1, blocking collectives, per_device(): columns = lax.all_to_all(columns, 'phase', 0, 0, tiled=True)  11.8 us
    all_to_all x1, starting transfers between devices, per_device(): own = lax.all_to_all(message, ('core', 'phase'), 0, 0, tiled=True)  9.29 us
    all_to_all x1, waiting for transfers between devices, per_device(): own = lax.all_to_all(message, ('core', 'phase'), 0, 0, tiled=True)  8.5 us
    ppermute x1, waiting for transfers between devices, per_device(): far = lax.ppermute(far, devices, pairs(-1))  5.68 us
    ppermute x1, starting transfers between devices, per_device(): near = lax.ppermute(near, devices, pairs(1))  5.48 us
    ppermute x1, starting transfers between devices, per_device(): far = lax.ppermute(far, devices, pairs(-1))  1.92 us
    pallas_call x1, Pallas kernels, pack(): pl.pallas_call(pack_kernel, out_shape=jax.ShapeDtypeStruct((2 * TILE * 4,...  1.56 us
  transfers between devices with their start and end apart: 3, of which 2 were waited for; matrix products, arithmetic and copies ran while one was open for 0% of the time, Pallas kernels for 0%

profile of v2, /device:TPU:64, one launch (start us, length us, event | category | flops | bytes accessed | tf_op | source)
XLA Modules:
  0.0 60.0 jit_solution(6217071850939387050)
XLA Ops:
  1.9 1.6 %pack.1 = f32[256,128]{1,0:T(8,128)} custom-call(s32[1]{0:T(128)} %bitcast.1.row_ref, f32[1]{0:T(128)S(6)} %copy.15.time_ref, f32[1]{0:T(128)S(6)} %copy.16.weight_ref, f32[32]{0:T(128)} %cor_ref.1, f32[3,8,128]{2,1,0:T(8,128)} %bitcast.17, f32[32,1024]{1,0:T(8,128)} %depth_ref.1, f32[24,128]{1,0:T(8,128)} %constant.26.clone.table_ref), custom_call_target="tpu_custom_call" | custom-call | tf_op jit(solution)/shard_map/pack/pallas_call | solution.py:292
  3.5 9.3 %all-to-all-start = ((f32[64,4,128]{2,1,0:T(4,128)}), f32[64,4,128]{2,1,0:T(4,128)S(1)}, u32[]{:S(2)}, u32[]{:S(2)}) async-start(f32[64,4,128]{2,1,0:T(4,128)} %bitcast.15), calls=%async_computation | async-start | bytes 262144 | tf_op jit(solution)/shard_map/all_to_all | solution.py:342
  12.8 8.5 %all-to-all-done = f32[64,4,128]{2,1,0:T(4,128)S(1)} async-done(((f32[64,4,128]{2,1,0:T(4,128)}), f32[64,4,128]{2,1,0:T(4,128)S(1)}, u32[]{:S(2)}, u32[]{:S(2)}) %all-to-all-start) | async-done | bytes 131104 | tf_op jit(solution)/shard_map/all_to_all | solution.py:342
  21.3 5.5 %collective-permute-start = (f32[136,128]{1,0:T(8,128)S(1)}, f32[136,128]{1,0:T(8,128)S(1)}, u32[]{:S(2)}, u32[]{:S(2)}) collective-permute-start(f32[136,128]{1,0:T(8,128)S(1)} %constant_dynamic-slice_fusion.1), channel_id=1, source_target_pairs={{0,2},{2,4},{4,6},{3,1},{5,3},{7,5},{8,10},{10,12},{12,14},{11,9},... | collective-permute-start | bytes 208904 | tf_op jit(solution)/shard_map/ppermute | solution.py:354
  26.8 1.9 %collective-permute-start.1 = (f32[8,128]{1,0:T(8,128)S(1)}, f32[8,128]{1,0:T(8,128)S(1)}, u32[]{:S(2)}, u32[]{:S(2)}) collective-permute-start(f32[8,128]{1,0:T(8,128)S(1)} %constant_dynamic-slice_fusion), channel_id=1, source_target_pairs={{2,0},{4,2},{6,4},{1,3},{3,5},{5,7},{10,8},{12,10},{14,12},{9,11},... | collective-permute-start | bytes 12296 | tf_op jit(solution)/shard_map/ppermute | solution.py:355
  28.8 5.7 %collective-permute-done.1.far_ref = f32[8,128]{1,0:T(8,128)S(1)} collective-permute-done((f32[8,128]{1,0:T(8,128)S(1)}, f32[8,128]{1,0:T(8,128)S(1)}, u32[]{:S(2)}, u32[]{:S(2)}) %collective-permute-start.1) | collective-permute-done | bytes 4128 | tf_op jit(solution)/shard_map/ppermute | solution.py:355
  34.4 0.0 collective-permute-done.near_ref
  34.4 12.3 %tile.1 = f32[32,128]{1,0:T(8,128)S(1)} custom-call(s32[1]{0:T(128)} %bitcast.place_ref, f32[256,128]{1,0:T(8,128)S(1)} %bitcast.13, f32[136,128]{1,0:T(8,128)S(1)} %collective-permute-done.near_ref, f32[8,128]{1,0:T(8,128)S(1)} %collective-permute-done.1.far_ref), custom_call_target="tpu_custom_call" | custom-call | tf_op jit(solution)/shard_map/tile/pallas_call | solution.py:301
  46.8 11.8 %all_to_all.22 = f32[32,1,128]{2,1,0:T(1,128)} all-to-all(f32[32,1,128]{2,1,0:T(1,128)S(1)} %bitcast.14), channel_id=1, replica_groups=mesh['phase'=32,'ring'=4,'core'=2] {'phase'}, dimensions={0} | all-to-all | bytes 32768 | tf_op jit(solution)/shard_map/all_to_all | solution.py:357
  58.6 1.4 %unpack.1 = (f32[3,8,128]{2,1,0:T(8,128)}, f32[3,8,128]{2,1,0:T(8,128)}) custom-call(f32[32,128]{1,0:T(8,128)} %bitcast.16, f32[3,8,128]{2,1,0:T(8,128)} %bitcast.18), custom_call_target="tpu_custom_call" | custom-call | tf_op jit(solution)/shard_map/unpack/pallas_call | solution.py:327
  (2 shorter events, 0.0 us)
Async XLA Ops:
  3.5 17.8 %all-to-all-start = ((f32[64,4,128]{2,1,0:T(4,128)}), f32[64,4,128]{2,1,0:T(4,128)S(1)}, u32[]{:S(2)}, u32[]{:S(2)}) async-start(f32[64,4,128]{2,1,0:T(4,128)} %bitcast.15), calls=%async_computation | async-start | bytes 262144 | tf_op jit(solution)/shard_map/all_to_all | solution.py:342
  21.3 13.1 %collective-permute-start = (f32[136,128]{1,0:T(8,128)S(1)}, f32[136,128]{1,0:T(8,128)S(1)}, u32[]{:S(2)}, u32[]{:S(2)}) collective-permute-start(f32[136,128]{1,0:T(8,128)S(1)} %constant_dynamic-slice_fusion.1), channel_id=1, source_target_pairs={{0,2},{2,4},{4,6},{3,1},{5,3},{7,5},{8,10},{10,12},{12,14},{11,9},... | collective-permute-start | bytes 208904 | tf_op jit(solution)/shard_map/ppermute | solution.py:354
  26.8 7.6 %collective-permute-start.1 = (f32[8,128]{1,0:T(8,128)S(1)}, f32[8,128]{1,0:T(8,128)S(1)}, u32[]{:S(2)}, u32[]{:S(2)}) collective-permute-start(f32[8,128]{1,0:T(8,128)S(1)} %constant_dynamic-slice_fusion), channel_id=1, source_target_pairs={{2,0},{4,2},{6,4},{1,3},{3,5},{5,7},{10,8},{12,10},{14,12},{9,11},... | collective-permute-start | bytes 12296 | tf_op jit(solution)/shard_map/ppermute | solution.py:355

commit v3 on v2

--- a/solution.py
+++ b/solution.py
@@ -24,6 +24,11 @@
 PAD = 8
 ROWS = PAD + 8 * BLOCKS + PAD
 WIDE = 3 * LANES
+EXTRA = False
+PIPELINED = True
+SENT = 5 * LANES if EXTRA else WIDE
+W_ROWS = 8 * 9 + 16
+TILE_SHAPES = [(256, 128), (136, 128), (8, 128)]
 SAMPLES = 32
 
 f32 = jnp.float32
@@ -115,11 +120,11 @@
         p_ref[k, ROWS - PAD - 8 : ROWS, :] = jnp.zeros((PAD + 8, WIDE), f32)
     p_ref[TERMS] = jnp.zeros((ROWS, WIDE), f32)
     for k in range(TERMS):
-        for block in (0, BLOCKS - 1):
-            z_ref[k, rows(block), :] = jnp.zeros((8, WIDE), f32)
+        z_ref[k, 0 : PAD + 16, :] = jnp.zeros((PAD + 16, WIDE), f32)
+        z_ref[k, ROWS - PAD - 16 : ROWS, :] = jnp.zeros((PAD + 16, WIDE), f32)
     for s in range(SAMPLES):
-        for block in (0, BLOCKS - 1):
-            w_ref[s, rows(block), :] = jnp.zeros((8, WIDE), f32)
+        w_ref[s, 0:8, :] = jnp.zeros((8, SENT), f32)
+        w_ref[s, W_ROWS - 8 : W_ROWS, :] = jnp.zeros((8, SENT), f32)
     for ref in (depth_ref, cor_ref):
         ref[0 : PAD + 8, :] = jnp.zeros((PAD + 8, LANES), f32)
         ref[ROWS - PAD - 8 : ROWS, :] = jnp.zeros((PAD + 8, LANES), f32)
@@ -196,9 +201,15 @@
         for f in range(3):
             ref[k, rows(block), f * LANES : (f + 1) * LANES] = values[f]
 
-    def averaged(outer, inner):
+    centre = lax.broadcasted_iota(jnp.int32, (8, LANES), 1)
+    centre = (centre >= LANES // 4) & (centre < 3 * LANES // 4)
+
+    def blocks(low, high):
+        return range(low // 8, high // 8 + 1)
+
+    def chebyshev(low, high):
         for k in range(1, TERMS):
-            for block in range(*outer):
+            for block in blocks(low + k, high - k):
                 new = operator(p_ref, k - 1, block)
                 if k == 1:
                     new = [0.5 * value for value in new]
@@ -206,48 +217,92 @@
                     new = [a + b for a, b in zip(new, fields(p_ref, k - 2, block))]
                 store(p_ref, k, block, new)
 
-        first, last = inner
-        for block in range(first, last):
-            value = p_ref[:, rows(block), :].reshape(80, WIDE)
-            high, low = split(value)
-            stacked = jnp.concatenate([high, low, high, jnp.zeros((16, WIDE), bf16)], axis=0)
-            waves = jnp.dot(forward_ref[...], stacked, preferred_element_type=f32)
-            w_ref[:, rows(block), :] = waves.reshape(SAMPLES, 8, WIDE)
-
-        def advect(s, block):
-            mid, up, down = rows(block), rows(block, 1), rows(block, -1)
-            h_at, u_at, v_at = slice(0, LANES), slice(LANES, 2 * LANES), slice(2 * LANES, WIDE)
-            h, u, v = w_ref[s, mid, h_at], w_ref[s, mid, u_at], w_ref[s, mid, v_at]
-            v_up, v_down = w_ref[s, up, v_at], w_ref[s, down, v_at]
-            out_h = east(h * u) + (w_ref[s, up, h_at] * v_up - w_ref[s, down, h_at] * v_down)
-            out_u = u * east(u) + v * (w_ref[s, up, u_at] - w_ref[s, down, u_at])
-            out_v = u * east(v) + v * (v_up - v_down)
-            return out_h, out_u, out_v
-
-        def pair(n, carry):
-            for block in range(first, last):
-                one, two = advect(2 * n, block), advect(2 * n + 1, block)
-                for f in range(3):
-                    high, low = split(jnp.concatenate([one[f], two[f]], axis=0))
-                    yh_ref[block, n, :, f * LANES : (f + 1) * LANES] = high
-                    yl_ref[block, n, :, f * LANES : (f + 1) * LANES] = low
-            return carry
-
-        lax.fori_loop(0, SAMPLES // 2, pair, 0)
-
-        for block in range(first, last):
-            high = yh_ref[block].reshape(256, WIDE)
-            low = yl_ref[block].reshape(256, WIDE)
-            both = jnp.dot(backh_ref[...], high, preferred_element_type=f32)
-            total = both[0:80] + both[80:160] + jnp.dot(backl_ref[...], low, preferred_element_type=f32)
-            total = total * -0.5
-            for k in range(TERMS):
-                term_at = total[8 * k : 8 * k + 8]
-                z_ref[k, rows(block), 0:LANES] = term_at[:, 0:LANES] * mask_ref[rows(block), :]
-                z_ref[k, rows(block), LANES:WIDE] = term_at[:, LANES:WIDE]
-
+    def terms_at(row):
+        return p_ref[:, PAD + row : PAD + row + 8, :]
+
+    def wave(n, left, right):
+        values = [terms_at(left)[:, :, f * LANES : (f + 1) * LANES].reshape(80, LANES) for f in range(3)]
+        if right is not None:
+            inside = jnp.concatenate([centre] * 10, axis=0)
+            for f in range(3):
+                other = terms_at(right)[:, :, f * LANES : (f + 1) * LANES].reshape(80, LANES)
+                values[f] = jnp.where(inside, values[f], pltpu.roll(other, LANES // 2, 1))
+        if EXTRA:
+            values = values + [east(values[1]), east(values[2])]
+        high, low = split(jnp.concatenate(values, axis=1))
+        stacked = jnp.concatenate([high, low, high, jnp.zeros((16, SENT), bf16)], axis=0)
+        waves = jnp.dot(forward_ref[...], stacked, preferred_element_type=f32)
+        w_ref[:, 8 + 8 * n : 16 + 8 * n, :] = waves.reshape(SAMPLES, 8, SENT)
+
+    def advect(s, n):
+        def at(f, offset=0):
+            return w_ref[s, 8 + 8 * n + offset : 16 + 8 * n + offset, f * LANES : (f + 1) * LANES]
+
+        h, u, v = at(0), at(1), at(2)
+        v_up, v_down = at(2, 1), at(2, -1)
+        u_east, v_east = (at(3), at(4)) if EXTRA else (east(u), east(v))
+        out_h = east(h * u) + (at(0, 1) * v_up - at(0, -1) * v_down)
+        out_u = u * u_east + v * (at(1, 1) - at(1, -1))
+        out_v = u * v_east + v * (v_up - v_down)
+        return out_h, out_u, out_v
+
+    def pulled(pair, n):
+        one, two = advect(2 * pair, n), advect(2 * pair + 1, n)
+        for f in range(3):
+            high, low = split(jnp.concatenate([one[f], two[f]], axis=0))
+            yh_ref[n, pair, :, f * LANES : (f + 1) * LANES] = high
+            yl_ref[n, pair, :, f * LANES : (f + 1) * LANES] = low
+
+    def weighted(n):
+        both = jnp.dot(backh_ref[...], yh_ref[n].reshape(256, WIDE), preferred_element_type=f32)
+        low = jnp.dot(backl_ref[...], yl_ref[n].reshape(256, WIDE), preferred_element_type=f32)
+        return (both[0:80] + both[80:160] + low) * -0.5
+
+    def put(total, row, first, last, turn):
+        at = slice(PAD + row + first, PAD + row + last)
+        mask = mask_ref[at, :]
+        for k in range(TERMS):
+            for f in range(3):
+                value = total[8 * k : 8 * k + 8, f * LANES : (f + 1) * LANES]
+                if turn:
+                    value = pltpu.roll(value, LANES // 2, 1)
+                value = value[first:last]
+                z_ref[k, at, f * LANES : (f + 1) * LANES] = value * mask if f == 0 else value
+
+    def mid(plan):
+        count = len(plan)
+
+        def finish(n):
+            total = weighted(n)
+            for row, first, last, turn in plan[n][2]:
+                put(total, row, first, last, turn)
+
+        if PIPELINED:
+            wave(0, *plan[0][:2])
+            for n in range(count):
+                if n + 1 < count:
+                    wave(n + 1, *plan[n + 1][:2])
+                for pair in range(SAMPLES // 2):
+                    pulled(pair, n)
+                if n > 0:
+                    finish(n - 1)
+            finish(count - 1)
+        else:
+            for n in range(count):
+                wave(n, *plan[n][:2])
+
+            def pairs(pair, carry):
+                for n in range(count):
+                    pulled(pair, n)
+                return carry
+
+            lax.fori_loop(0, SAMPLES // 2, pairs, 0)
+            for n in range(count):
+                finish(n)
+
+    def clenshaw(low, high):
         for k in range(DEG - 1, -1, -1):
-            for block in range(first, last):
+            for block in blocks(low - k, high + k):
                 new = operator(z_ref, k + 1, block)
                 if k == 0:
                     new = [0.5 * value for value in new]
@@ -256,12 +311,26 @@
                     new = [a + b for a, b in zip(new, fields(z_ref, k + 2, block))]
                 store(z_ref, k, block, new)
 
-    averaged((0, 13), (1, 12))
+    chebyshev(2, 101)
+    mid(
+        [(24 + 8 * n, None, [(24 + 8 * n, 1 if n == 0 else 0, 7 if n == 6 else 8, False)]) for n in range(7)]
+        + [(10, 78, [(10, 1, 8, False), (78, 1, 8, True)]), (18, 86, [(18, 0, 7, False), (86, 0, 7, True)])]
+    )
+    clenshaw(19, 84)
     for block in range(2, 11):
         at = rows(block)
         t_ref[at, :] = z_ref[0, at, :]
         p_ref[0, at, :] = p_ref[0, at, :] + STEP * z_ref[0, at, :]
-    averaged((2, 11), (3, 10))
+    chebyshev(19, 84)
+    mid(
+        [
+            (24, 48, [(24, 0, 8, False), (48, 4, 8, True)]),
+            (32, 56, [(32, 0, 8, False), (56, 0, 8, True)]),
+            (40, 64, [(40, 0, 8, False), (64, 0, 8, True)]),
+            (48, 72, [(48, 0, 4, False), (72, 0, 8, True)]),
+        ]
+    )
+    clenshaw(36, 67)
     at = slice(PAD + BASE, PAD + BASE + TILE)
     tendency = 0.5 * (t_ref[at, :] + z_ref[0, at, :])
     lanes = lax.broadcasted_iota(jnp.int32, (TILE, LANES), 1)
@@ -306,7 +375,7 @@
         scratch_shapes=[
             pltpu.VMEM((TERMS + 1, ROWS, WIDE), f32),
             pltpu.VMEM((TERMS, ROWS, WIDE), f32),
-            pltpu.VMEM((SAMPLES, ROWS, WIDE), f32),
+            pltpu.VMEM((SAMPLES, W_ROWS, SENT), f32),
             pltpu.VMEM((BLOCKS, SAMPLES // 2, 16, WIDE), bf16),
             pltpu.VMEM((BLOCKS, SAMPLES // 2, 16, WIDE), bf16),
             pltpu.VMEM((ROWS, WIDE), f32),
@@ -341,18 +410,12 @@
     message = pack(row[None], phase_times, phase_weights, coriolis, state, ocean_depth)
     own = lax.all_to_all(message, ("core", "phase"), 0, 0, tiled=True)
     devices = ("phase", "ring", "core")
-
-    def index(phase, at, of):
-        return (phase * ring + at) * 2 + of
-
-    def pairs(step):
-        moves = [(at, at + step, 0) for at in range(ring)] + [(at, at - step, 1) for at in range(ring)]
-        return [(index(p, a, c), index(p, b, c)) for p in range(TILE) for a, b, c in moves if 0 <= b < ring]
-
+    moves = [(at, at + 1, 0) for at in range(ring - 1)] + [(at + 1, at, 1) for at in range(ring - 1)]
+    pairs = [((p * ring + a) * 2 + c, (p * ring + b) * 2 + c) for p in range(TILE) for a, b, c in moves]
     near = lax.dynamic_slice_in_dim(own, jnp.where(core == 0, 4 * (TILE - 2), 0), 4 * (TILE + 2), 0)
-    far = lax.dynamic_slice_in_dim(own, jnp.where(core == 0, 0, 4 * (2 * TILE - 2)), 8, 0)
-    near = lax.ppermute(near, devices, pairs(1))
-    far = lax.ppermute(far, devices, pairs(-1))
+    near = lax.ppermute(near, devices, pairs)
+    far = lax.dynamic_slice_in_dim(near, jnp.where(core == 0, 4 * TILE, 0), 8, 0)
+    far = lax.ppermute(far, "core", [(0, 1), (1, 0)])
     columns = tile(lat[None], own, near, far)
     columns = lax.all_to_all(columns, "phase", 0, 0, tiled=True)
     state_next, tendency = unpack(columns, state)

time: 60.4 us -> 51.8 us (0.86)
  Pallas kernels: 15.3 us -> 10.9 us
  waiting for transfers between devices: 14.2 us -> 11.2 us
  starting transfers between devices: 16.7 us -> 15.4 us
    pallas_call x1, Pallas kernels: 12.3 us -> 7.93 us  [tile(): pl.pallas_call(tile_kernel, out_shape=jax.ShapeDtypeStruct((TILE, LANES),...]
    ppermute x2, waiting for transfers between devices: 5.68 us -> 2.74 us  [the longest x1 1.92 us: per_device(): near = lax.ppermute(near, devices, pairs)]
    ppermute x2, starting transfers between devices: 7.4 us -> 6.08 us  [the longest x1 5.48 us: per_device(): near = lax.ppermute(near, devices, pairs)]
  transfers between devices with their start and end apart: 3 -> 3, of which waited for: 2 -> 3; matrix products, arithmetic and copies ran while one was open for 0% -> 0% of each run, Pallas kernels for 0% -> 0%
where the time goes in v3:
time: 51.8 us; the launch traced here: 51.4 us
  starting transfers between devices  15.4 us (30%)
  blocking collectives  11.9 us (23%)
  waiting for transfers between devices  11.2 us (22%)
  Pallas kernels  10.9 us (21%)
  between operations  1.97 us (4%)
    all_to_all x1, blocking collectives, per_device(): columns = lax.all_to_all(columns, 'phase', 0, 0, tiled=True)  11.9 us
    all_to_all x1, starting transfers between devices, per_device(): own = lax.all_to_all(message, ('core', 'phase'), 0, 0, tiled=True)  9.29 us
    all_to_all x1, waiting for transfers between devices, per_device(): own = lax.all_to_all(message, ('core', 'phase'), 0, 0, tiled=True)  8.51 us
    pallas_call x1, Pallas kernels, tile(): pl.pallas_call(tile_kernel, out_shape=jax.ShapeDtypeStruct((TILE, LANES),...  7.93 us
    ppermute x1, starting transfers between devices, per_device(): near = lax.ppermute(near, devices, pairs)  5.48 us
    ppermute x1, waiting for transfers between devices, per_device(): near = lax.ppermute(near, devices, pairs)  1.92 us
    pallas_call x1, Pallas kernels, pack(): pl.pallas_call(pack_kernel, out_shape=jax.ShapeDtypeStruct((2 * TILE * 4,...  1.56 us
    pallas_call x1, Pallas kernels, unpack(): pl.pallas_call(unpack_kernel, out_shape=(shape, shape), in_specs=[vmem(),...  1.41 us
  transfers between devices with their start and end apart: 3, of which 3 were waited for; matrix products, arithmetic and copies ran while one was open for 0% of the time, Pallas kernels for 0%

profile of v3, /device:TPU:64, one launch (start us, length us, event | category | flops | bytes accessed | tf_op | source)
XLA Modules:
  0.0 51.4 jit_solution(4816475997072505702)
XLA Ops:
  1.9 1.6 %pack.1 = f32[256,128]{1,0:T(8,128)} custom-call(s32[1]{0:T(128)} %bitcast.1.row_ref, f32[1]{0:T(128)S(6)} %copy.15.time_ref, f32[1]{0:T(128)S(6)} %copy.16.weight_ref, f32[32]{0:T(128)} %cor_ref.1, f32[3,8,128]{2,1,0:T(8,128)} %bitcast.16, f32[32,1024]{1,0:T(8,128)} %depth_ref.1, f32[24,128]{1,0:T(8,128)} %constant.27.clone.table_ref), custom_call_target="tpu_custom_call" | custom-call | tf_op jit(solution)/shard_map/pack/pallas_call | solution.py:361
  3.5 9.3 %all-to-all-start = ((f32[64,4,128]{2,1,0:T(4,128)}), f32[64,4,128]{2,1,0:T(4,128)S(1)}, u32[]{:S(2)}, u32[]{:S(2)}) async-start(f32[64,4,128]{2,1,0:T(4,128)} %bitcast.14), calls=%async_computation | async-start | bytes 262144 | tf_op jit(solution)/shard_map/all_to_all | solution.py:411
  12.8 8.5 %all-to-all-done = f32[64,4,128]{2,1,0:T(4,128)S(1)} async-done(((f32[64,4,128]{2,1,0:T(4,128)}), f32[64,4,128]{2,1,0:T(4,128)S(1)}, u32[]{:S(2)}, u32[]{:S(2)}) %all-to-all-start) | async-done | bytes 131104 | tf_op jit(solution)/shard_map/all_to_all | solution.py:411
  21.3 5.5 %collective-permute-start = (f32[136,128]{1,0:T(8,128)S(1)}, f32[136,128]{1,0:T(8,128)S(1)}, u32[]{:S(2)}, u32[]{:S(2)}) collective-permute-start(f32[136,128]{1,0:T(8,128)S(1)} %constant_dynamic-slice_fusion.1), channel_id=1, source_target_pairs={{0,2},{2,4},{4,6},{3,1},{5,3},{7,5},{8,10},{10,12},{12,14},{11,9},... | collective-permute-start | bytes 208904 | tf_op jit(solution)/shard_map/ppermute | solution.py:416
  26.8 1.9 %collective-permute-done.near_ref = f32[136,128]{1,0:T(8,128)S(1)} collective-permute-done((f32[136,128]{1,0:T(8,128)S(1)}, f32[136,128]{1,0:T(8,128)S(1)}, u32[]{:S(2)}, u32[]{:S(2)}) %collective-permute-start) | collective-permute-done | bytes 69664 | tf_op jit(solution)/shard_map/ppermute | solution.py:416
  28.7 0.6 %collective-permute-start.1 = (f32[8,128]{1,0:T(8,128)S(1)}, f32[8,128]{1,0:T(8,128)S(1)}, u32[]{:S(2)}, u32[]{:S(2)}) collective-permute-start(f32[8,128]{1,0:T(8,128)S(1)} %constant_dynamic-slice_fusion), channel_id=1, source_target_pairs={{0,1},{1,0},{2,3},{3,2},{4,5},{5,4},{6,7},{7,6},{8,9},{9,8},{10,11... | collective-permute-start | bytes 12296 | tf_op jit(solution)/shard_map/ppermute | solution.py:418
  29.3 0.8 %collective-permute-done.1.far_ref = f32[8,128]{1,0:T(8,128)S(1)} collective-permute-done((f32[8,128]{1,0:T(8,128)S(1)}, f32[8,128]{1,0:T(8,128)S(1)}, u32[]{:S(2)}, u32[]{:S(2)}) %collective-permute-start.1) | collective-permute-done | bytes 4128 | tf_op jit(solution)/shard_map/ppermute | solution.py:418
  30.2 7.9 %tile.1 = f32[32,128]{1,0:T(8,128)S(1)} custom-call(s32[1]{0:T(128)} %bitcast.place_ref, f32[256,128]{1,0:T(8,128)S(1)} %bitcast.12, f32[136,128]{1,0:T(8,128)S(1)} %collective-permute-done.near_ref, f32[8,128]{1,0:T(8,128)S(1)} %collective-permute-done.1.far_ref), custom_call_target="tpu_custom_call" | custom-call | tf_op jit(solution)/shard_map/tile/pallas_call | solution.py:370
  38.1 11.9 %all_to_all.22 = f32[32,1,128]{2,1,0:T(1,128)} all-to-all(f32[32,1,128]{2,1,0:T(1,128)S(1)} %bitcast.13), channel_id=1, replica_groups=mesh['phase'=32,'ring'=4,'core'=2] {'phase'}, dimensions={0} | all-to-all | bytes 32768 | tf_op jit(solution)/shard_map/all_to_all | solution.py:420
  50.0 1.4 %unpack.1 = (f32[3,8,128]{2,1,0:T(8,128)}, f32[3,8,128]{2,1,0:T(8,128)}) custom-call(f32[32,128]{1,0:T(8,128)} %bitcast.15, f32[3,8,128]{2,1,0:T(8,128)} %bitcast.17), custom_call_target="tpu_custom_call" | custom-call | tf_op jit(solution)/shard_map/unpack/pallas_call | solution.py:396
  (2 shorter events, 0.0 us)
Async XLA Ops:
  3.5 17.8 %all-to-all-start = ((f32[64,4,128]{2,1,0:T(4,128)}), f32[64,4,128]{2,1,0:T(4,128)S(1)}, u32[]{:S(2)}, u32[]{:S(2)}) async-start(f32[64,4,128]{2,1,0:T(4,128)} %bitcast.14), calls=%async_computation | async-start | bytes 262144 | tf_op jit(solution)/shard_map/all_to_all | solution.py:411
  21.3 7.4 %collective-permute-start = (f32[136,128]{1,0:T(8,128)S(1)}, f32[136,128]{1,0:T(8,128)S(1)}, u32[]{:S(2)}, u32[]{:S(2)}) collective-permute-start(f32[136,128]{1,0:T(8,128)S(1)} %constant_dynamic-slice_fusion.1), channel_id=1, source_target_pairs={{0,2},{2,4},{4,6},{3,1},{5,3},{7,5},{8,10},{10,12},{12,14},{11,9},... | collective-permute-start | bytes 208904 | tf_op jit(solution)/shard_map/ppermute | solution.py:416
  28.7 1.4 %collective-permute-start.1 = (f32[8,128]{1,0:T(8,128)S(1)}, f32[8,128]{1,0:T(8,128)S(1)}, u32[]{:S(2)}, u32[]{:S(2)}) collective-permute-start(f32[8,128]{1,0:T(8,128)S(1)} %constant_dynamic-slice_fusion), channel_id=1, source_target_pairs={{0,1},{1,0},{2,3},{3,2},{4,5},{5,4},{6,7},{7,6},{8,9},{9,8},{10,11... | collective-permute-start | bytes 12296 | tf_op jit(solution)/shard_map/ppermute | solution.py:418

commit v4 on v3

--- a/solution.py
+++ b/solution.py
@@ -46,8 +46,8 @@
 def pack_kernel(row_ref, time_ref, weight_ref, cor_ref, state_ref, depth_ref, table_ref, out_ref, line_ref):
     row = row_ref[0]
     lane = lax.broadcasted_iota(jnp.int32, (1, LANES), 1)
-    half = time_ref[0] * 0.5
-    square = jnp.full((1, LANES), half * half, f32)
+    half = jnp.broadcast_to(time_ref[...] * 0.5, (1, LANES))
+    square = half * half
     total = jnp.zeros((1, LANES), f32)
     power = jnp.ones((1, LANES), f32)
     for m in range(SERIES):
@@ -58,7 +58,7 @@
         scale = jnp.where((lane >= k) & (lane < TERMS), scale * half, scale)
     forward = total * scale
     forward = jnp.where(lane == 0, forward, 2.0 * forward)
-    backward = jnp.where(lane % 2 == 0, forward, -forward) * weight_ref[0]
+    backward = jnp.where(lane % 2 == 0, forward, -forward) * jnp.broadcast_to(weight_ref[...], (1, LANES))
     cor = jnp.full((1, LANES), cor_ref[row], f32)
     lanes = lax.broadcasted_iota(jnp.int32, (8, LANES), 1)
     mine = lax.broadcasted_iota(jnp.int32, (8, LANES), 0) == lax.rem(row, 8)
@@ -115,16 +115,16 @@
         start = PAD + 8 * block + offset
         return slice(start, start + 8 * count)
 
-    for k in range(TERMS + 1):
-        p_ref[k, 0 : PAD + 8, :] = jnp.zeros((PAD + 8, WIDE), f32)
-        p_ref[k, ROWS - PAD - 8 : ROWS, :] = jnp.zeros((PAD + 8, WIDE), f32)
-    p_ref[TERMS] = jnp.zeros((ROWS, WIDE), f32)
+    edge = jnp.zeros((3, PAD + 8, LANES), f32)
     for k in range(TERMS):
-        z_ref[k, 0 : PAD + 16, :] = jnp.zeros((PAD + 16, WIDE), f32)
-        z_ref[k, ROWS - PAD - 16 : ROWS, :] = jnp.zeros((PAD + 16, WIDE), f32)
+        p_ref[k, :, 0 : PAD + 8, :] = edge
+        p_ref[k, :, ROWS - PAD - 8 : ROWS, :] = edge
+        z_ref[k, :, PAD : PAD + 16, :] = edge
+        z_ref[k, :, ROWS - PAD - 16 : ROWS - PAD, :] = edge
+    p_ref[TERMS] = jnp.zeros((3, ROWS, LANES), f32)
     for s in range(SAMPLES):
-        w_ref[s, 0:8, :] = jnp.zeros((8, SENT), f32)
-        w_ref[s, W_ROWS - 8 : W_ROWS, :] = jnp.zeros((8, SENT), f32)
+        w_ref[s, :, 0:8, :] = edge[:, :8] if not EXTRA else jnp.zeros((5, 8, LANES), f32)
+        w_ref[s, :, W_ROWS - 8 : W_ROWS, :] = edge[:, :8] if not EXTRA else jnp.zeros((5, 8, LANES), f32)
     for ref in (depth_ref, cor_ref):
         ref[0 : PAD + 8, :] = jnp.zeros((PAD + 8, LANES), f32)
         ref[ROWS - PAD - 8 : ROWS, :] = jnp.zeros((PAD + 8, LANES), f32)
@@ -132,9 +132,9 @@
     def place(ref, count, at):
         at = PAD + BASE + at
         h, u, v, depth, = [ref[pl.ds(f, count, stride=4), :] for f in range(4)]
-        p_ref[0, at : at + count, 0:LANES] = h
-        p_ref[0, at : at + count, LANES : 2 * LANES] = u
-        p_ref[0, at : at + count, 2 * LANES : WIDE] = v
+        p_ref[0, 0, at : at + count, :] = h
+        p_ref[0, 1, at : at + count, :] = u
+        p_ref[0, 2, at : at + count, :] = v
         depth_ref[at : at + count, :] = depth * 0.4
         cor_ref[at : at + count, :] = jnp.broadcast_to(depth[:, 0:1] * 0.8, (count, LANES))
 
@@ -185,21 +185,20 @@
 
     def operator(ref, k, block):
         mid, up, down = rows(block), rows(block, 1), rows(block, -1)
-        h_at, u_at, v_at = slice(0, LANES), slice(LANES, 2 * LANES), slice(2 * LANES, WIDE)
-        h, u, v = ref[k, mid, h_at], ref[k, mid, u_at], ref[k, mid, v_at]
+        h, u, v = ref[k, 0, mid, :], ref[k, 1, mid, :], ref[k, 2, mid, :]
         mask, cor = mask_ref[mid, :], cor_ref[mid, :]
-        flux = east(depth_ref[mid, :] * u) + (depth_ref[up, :] * ref[k, up, v_at] - depth_ref[down, :] * ref[k, down, v_at])
+        flux = east(depth_ref[mid, :] * u) + (depth_ref[up, :] * ref[k, 2, up, :] - depth_ref[down, :] * ref[k, 2, down, :])
         out_h = -(mask * flux)
         out_u = cor * v - 0.4 * east(h)
-        out_v = mask * (-0.4 * (ref[k, up, h_at] - ref[k, down, h_at])) - cor * u
+        out_v = mask * (-0.4 * (ref[k, 0, up, :] - ref[k, 0, down, :])) - cor * u
         return out_h, out_u, out_v
 
     def fields(ref, k, block):
-        return [ref[k, rows(block), f * LANES : (f + 1) * LANES] for f in range(3)]
+        return [ref[k, f, rows(block), :] for f in range(3)]
 
     def store(ref, k, block, values):
         for f in range(3):
-            ref[k, rows(block), f * LANES : (f + 1) * LANES] = values[f]
+            ref[k, f, rows(block), :] = values[f]
 
     centre = lax.broadcasted_iota(jnp.int32, (8, LANES), 1)
     centre = (centre >= LANES // 4) & (centre < 3 * LANES // 4)
@@ -217,26 +216,26 @@
                     new = [a + b for a, b in zip(new, fields(p_ref, k - 2, block))]
                 store(p_ref, k, block, new)
 
-    def terms_at(row):
-        return p_ref[:, PAD + row : PAD + row + 8, :]
+    def terms_at(f, row):
+        return p_ref[:, f, PAD + row : PAD + row + 8, :].reshape(80, LANES)
 
     def wave(n, left, right):
-        values = [terms_at(left)[:, :, f * LANES : (f + 1) * LANES].reshape(80, LANES) for f in range(3)]
+        values = [terms_at(f, left) for f in range(3)]
         if right is not None:
             inside = jnp.concatenate([centre] * 10, axis=0)
             for f in range(3):
-                other = terms_at(right)[:, :, f * LANES : (f + 1) * LANES].reshape(80, LANES)
-                values[f] = jnp.where(inside, values[f], pltpu.roll(other, LANES // 2, 1))
+                values[f] = jnp.where(inside, values[f], pltpu.roll(terms_at(f, right), LANES // 2, 1))
         if EXTRA:
             values = values + [east(values[1]), east(values[2])]
         high, low = split(jnp.concatenate(values, axis=1))
         stacked = jnp.concatenate([high, low, high, jnp.zeros((16, SENT), bf16)], axis=0)
         waves = jnp.dot(forward_ref[...], stacked, preferred_element_type=f32)
-        w_ref[:, 8 + 8 * n : 16 + 8 * n, :] = waves.reshape(SAMPLES, 8, SENT)
+        for f in range(len(values)):
+            w_ref[:, f, 8 + 8 * n : 16 + 8 * n, :] = waves[:, f * LANES : (f + 1) * LANES].reshape(SAMPLES, 8, LANES)
 
     def advect(s, n):
         def at(f, offset=0):
-            return w_ref[s, 8 + 8 * n + offset : 16 + 8 * n + offset, f * LANES : (f + 1) * LANES]
+            return w_ref[s, f, 8 + 8 * n + offset : 16 + 8 * n + offset, :]
 
         h, u, v = at(0), at(1), at(2)
         v_up, v_down = at(2, 1), at(2, -1)
@@ -267,7 +266,7 @@
                 if turn:
                     value = pltpu.roll(value, LANES // 2, 1)
                 value = value[first:last]
-                z_ref[k, at, f * LANES : (f + 1) * LANES] = value * mask if f == 0 else value
+                z_ref[k, f, at, :] = value * mask if f == 0 else value
 
     def mid(plan):
         count = len(plan)
@@ -319,8 +318,8 @@
     clenshaw(19, 84)
     for block in range(2, 11):
         at = rows(block)
-        t_ref[at, :] = z_ref[0, at, :]
-        p_ref[0, at, :] = p_ref[0, at, :] + STEP * z_ref[0, at, :]
+        t_ref[:, at, :] = z_ref[0, :, at, :]
+        p_ref[0, :, at, :] = p_ref[0, :, at, :] + STEP * z_ref[0, :, at, :]
     chebyshev(19, 84)
     mid(
         [
@@ -332,9 +331,9 @@
     )
     clenshaw(36, 67)
     at = slice(PAD + BASE, PAD + BASE + TILE)
-    tendency = 0.5 * (t_ref[at, :] + z_ref[0, at, :])
+    tendency = 0.5 * (t_ref[:, at, :] + z_ref[0, :, at, :])
     lanes = lax.broadcasted_iota(jnp.int32, (TILE, LANES), 1)
-    parts = [pltpu.roll(tendency[:, f * LANES : (f + 1) * LANES], (TILE * f - LEFT) % LANES, 1) for f in range(3)]
+    parts = [pltpu.roll(tendency[f], (TILE * f - LEFT) % LANES, 1) for f in range(3)]
     out_ref[...] = jnp.where(lanes < TILE, parts[0], jnp.where(lanes < 2 * TILE, parts[1], parts[2]))
 
 
@@ -351,7 +350,7 @@
         num_scalar_prefetch=1,
         grid=(1,),
         in_specs=[
-            smem(), smem(), smem(), vmem(),
+            vmem(), vmem(), smem(), vmem(),
             pl.BlockSpec((8, NLON), lambda i, at: (lax.div(at[0], 8), 0)),
             vmem(),
         ],
@@ -363,7 +362,7 @@
         out_shape=jax.ShapeDtypeStruct((2 * TILE * 4, LANES), f32),
         grid_spec=grid,
         name="pack",
-    )(row, times, weights, cor, state, depth, jnp.asarray(series_table()))
+    )(row, times.reshape(1, 1), weights.reshape(1, 1), cor, state, depth, jnp.asarray(series_table()))
 
 
 def tile(place, own, near, far):
@@ -373,12 +372,12 @@
         in_specs=[smem()] + [vmem()] * 3,
         out_specs=vmem(),
         scratch_shapes=[
-            pltpu.VMEM((TERMS + 1, ROWS, WIDE), f32),
-            pltpu.VMEM((TERMS, ROWS, WIDE), f32),
-            pltpu.VMEM((SAMPLES, W_ROWS, SENT), f32),
+            pltpu.VMEM((TERMS + 1, 3, ROWS, LANES), f32),
+            pltpu.VMEM((TERMS, 3, ROWS, LANES), f32),
+            pltpu.VMEM((SAMPLES, SENT // LANES, W_ROWS, LANES), f32),
             pltpu.VMEM((BLOCKS, SAMPLES // 2, 16, WIDE), bf16),
             pltpu.VMEM((BLOCKS, SAMPLES // 2, 16, WIDE), bf16),
-            pltpu.VMEM((ROWS, WIDE), f32),
+            pltpu.VMEM((3, ROWS, LANES), f32),
             pltpu.VMEM((ROWS, LANES), f32),
             pltpu.VMEM((ROWS, LANES), f32),
             pltpu.VMEM((ROWS, LANES), f32),

time: 51.8 us -> 51.2 us (0.988)
  Pallas kernels: 10.9 us -> 10.3 us
    pallas_call x1, Pallas kernels: 7.93 us -> 7.28 us  [tile(): pl.pallas_call(tile_kernel, out_shape=jax.ShapeDtypeStruct((TILE, LANES),...]
where the time goes in v4:
time: 51.2 us; the launch traced here: 50.7 us
  starting transfers between devices  15.4 us (30%)
  blocking collectives  11.9 us (23%)
  waiting for transfers between devices  11.2 us (22%)
  Pallas kernels  10.3 us (20%)
  between operations  1.97 us (4%)
    all_to_all x1, blocking collectives, per_device(): columns = lax.all_to_all(columns, 'phase', 0, 0, tiled=True)  11.9 us
    all_to_all x1, starting transfers between devices, per_device(): own = lax.all_to_all(message, ('core', 'phase'), 0, 0, tiled=True)  9.29 us
    all_to_all x1, waiting for transfers between devices, per_device(): own = lax.all_to_all(message, ('core', 'phase'), 0, 0, tiled=True)  8.51 us
    pallas_call x1, Pallas kernels, tile(): pl.pallas_call(tile_kernel, out_shape=jax.ShapeDtypeStruct((TILE, LANES),...  7.28 us
    ppermute x1, starting transfers between devices, per_device(): near = lax.ppermute(near, devices, pairs)  5.48 us
    ppermute x1, waiting for transfers between devices, per_device(): near = lax.ppermute(near, devices, pairs)  1.92 us
    pallas_call x1, Pallas kernels, pack(): pl.pallas_call(pack_kernel, out_shape=jax.ShapeDtypeStruct((2 * TILE * 4,...  1.58 us
    pallas_call x1, Pallas kernels, unpack(): pl.pallas_call(unpack_kernel, out_shape=(shape, shape), in_specs=[vmem(),...  1.41 us
  transfers between devices with their start and end apart: 3, of which 3 were waited for; matrix products, arithmetic and copies ran while one was open for 0% of the time, Pallas kernels for 0%

profile of v4, /device:TPU:64, one launch (start us, length us, event | category | flops | bytes accessed | tf_op | source)
XLA Modules:
  0.0 50.7 jit_solution(5658550683046933477)
XLA Ops:
  1.9 1.6 %pack.1 = f32[256,128]{1,0:T(8,128)} custom-call(s32[1]{0:T(128)} %bitcast.1.row_ref, f32[1,1]{1,0:T(1,128)} %bitcast.13.time_ref, f32[1,1]{1,0:T(1,128)} %bitcast.14.weight_ref, f32[32]{0:T(128)} %cor_ref.1, f32[3,8,128]{2,1,0:T(8,128)} %bitcast.20, f32[32,1024]{1,0:T(8,128)} %depth_ref.1, f32[24,128]{1,0:T(8,128)} %constant.27.clone.table_ref), custom_call_target="tpu_custom_call" | custom-call | tf_op jit(solution)/shard_map/pack/pallas_call | solution.py:360
  3.5 9.3 %all-to-all-start = ((f32[64,4,128]{2,1,0:T(4,128)}), f32[64,4,128]{2,1,0:T(4,128)S(1)}, u32[]{:S(2)}, u32[]{:S(2)}) async-start(f32[64,4,128]{2,1,0:T(4,128)} %bitcast.18), calls=%async_computation | async-start | bytes 262144 | tf_op jit(solution)/shard_map/all_to_all | solution.py:410
  12.8 8.5 %all-to-all-done = f32[64,4,128]{2,1,0:T(4,128)S(1)} async-done(((f32[64,4,128]{2,1,0:T(4,128)}), f32[64,4,128]{2,1,0:T(4,128)S(1)}, u32[]{:S(2)}, u32[]{:S(2)}) %all-to-all-start) | async-done | bytes 131104 | tf_op jit(solution)/shard_map/all_to_all | solution.py:410
  21.3 5.5 %collective-permute-start = (f32[136,128]{1,0:T(8,128)S(1)}, f32[136,128]{1,0:T(8,128)S(1)}, u32[]{:S(2)}, u32[]{:S(2)}) collective-permute-start(f32[136,128]{1,0:T(8,128)S(1)} %constant_dynamic-slice_fusion.1), channel_id=1, source_target_pairs={{0,2},{2,4},{4,6},{3,1},{5,3},{7,5},{8,10},{10,12},{12,14},{11,9},... | collective-permute-start | bytes 208904 | tf_op jit(solution)/shard_map/ppermute | solution.py:415
  26.8 1.9 %collective-permute-done.near_ref = f32[136,128]{1,0:T(8,128)S(1)} collective-permute-done((f32[136,128]{1,0:T(8,128)S(1)}, f32[136,128]{1,0:T(8,128)S(1)}, u32[]{:S(2)}, u32[]{:S(2)}) %collective-permute-start) | collective-permute-done | bytes 69664 | tf_op jit(solution)/shard_map/ppermute | solution.py:415
  28.7 0.6 %collective-permute-start.1 = (f32[8,128]{1,0:T(8,128)S(1)}, f32[8,128]{1,0:T(8,128)S(1)}, u32[]{:S(2)}, u32[]{:S(2)}) collective-permute-start(f32[8,128]{1,0:T(8,128)S(1)} %constant_dynamic-slice_fusion), channel_id=1, source_target_pairs={{0,1},{1,0},{2,3},{3,2},{4,5},{5,4},{6,7},{7,6},{8,9},{9,8},{10,11... | collective-permute-start | bytes 12296 | tf_op jit(solution)/shard_map/ppermute | solution.py:417
  29.3 0.8 %collective-permute-done.1.far_ref = f32[8,128]{1,0:T(8,128)S(1)} collective-permute-done((f32[8,128]{1,0:T(8,128)S(1)}, f32[8,128]{1,0:T(8,128)S(1)}, u32[]{:S(2)}, u32[]{:S(2)}) %collective-permute-start.1) | collective-permute-done | bytes 4128 | tf_op jit(solution)/shard_map/ppermute | solution.py:417
  30.2 7.3 %tile.1 = f32[32,128]{1,0:T(8,128)S(1)} custom-call(s32[1]{0:T(128)} %bitcast.place_ref, f32[256,128]{1,0:T(8,128)S(1)} %bitcast.16, f32[136,128]{1,0:T(8,128)S(1)} %collective-permute-done.near_ref, f32[8,128]{1,0:T(8,128)S(1)} %collective-permute-done.1.far_ref), custom_call_target="tpu_custom_call" | custom-call | tf_op jit(solution)/shard_map/tile/pallas_call | solution.py:369
  37.5 11.9 %all_to_all.22 = f32[32,1,128]{2,1,0:T(1,128)} all-to-all(f32[32,1,128]{2,1,0:T(1,128)S(1)} %bitcast.17), channel_id=1, replica_groups=mesh['phase'=32,'ring'=4,'core'=2] {'phase'}, dimensions={0} | all-to-all | bytes 32768 | tf_op jit(solution)/shard_map/all_to_all | solution.py:419
  49.3 1.4 %unpack.1 = (f32[3,8,128]{2,1,0:T(8,128)}, f32[3,8,128]{2,1,0:T(8,128)}) custom-call(f32[32,128]{1,0:T(8,128)} %bitcast.19, f32[3,8,128]{2,1,0:T(8,128)} %bitcast.21), custom_call_target="tpu_custom_call" | custom-call | tf_op jit(solution)/shard_map/unpack/pallas_call | solution.py:395
  (2 shorter events, 0.0 us)
Async XLA Ops:
  3.5 17.8 %all-to-all-start = ((f32[64,4,128]{2,1,0:T(4,128)}), f32[64,4,128]{2,1,0:T(4,128)S(1)}, u32[]{:S(2)}, u32[]{:S(2)}) async-start(f32[64,4,128]{2,1,0:T(4,128)} %bitcast.18), calls=%async_computation | async-start | bytes 262144 | tf_op jit(solution)/shard_map/all_to_all | solution.py:410
  21.3 7.4 %collective-permute-start = (f32[136,128]{1,0:T(8,128)S(1)}, f32[136,128]{1,0:T(8,128)S(1)}, u32[]{:S(2)}, u32[]{:S(2)}) collective-permute-start(f32[136,128]{1,0:T(8,128)S(1)} %constant_dynamic-slice_fusion.1), channel_id=1, source_target_pairs={{0,2},{2,4},{4,6},{3,1},{5,3},{7,5},{8,10},{10,12},{12,14},{11,9},... | collective-permute-start | bytes 208904 | tf_op jit(solution)/shard_map/ppermute | solution.py:415
  28.7 1.4 %collective-permute-start.1 = (f32[8,128]{1,0:T(8,128)S(1)}, f32[8,128]{1,0:T(8,128)S(1)}, u32[]{:S(2)}, u32[]{:S(2)}) collective-permute-start(f32[8,128]{1,0:T(8,128)S(1)} %constant_dynamic-slice_fusion), channel_id=1, source_target_pairs={{0,1},{1,0},{2,3},{3,2},{4,5},{5,4},{6,7},{7,6},{8,9},{9,8},{10,11... | collective-permute-start | bytes 12296 | tf_op jit(solution)/shard_map/ppermute | solution.py:417

commit v5 on v4

--- a/solution.py
+++ b/solution.py
@@ -407,13 +407,16 @@
     core = lax.axis_index("core").astype(jnp.int32)
     lat = 2 * lax.axis_index("ring").astype(jnp.int32) + core
     message = pack(row[None], phase_times, phase_weights, coriolis, state, ocean_depth)
+    near_at = jnp.where(core == 0, 4 * (TILE - 2), 0).astype(jnp.uint32)
+    far_at = jnp.where(core == 0, 4 * TILE, 0).astype(jnp.uint32)
+    message, near_at, far_at, lat = lax.optimization_barrier((message, near_at, far_at, lat))
     own = lax.all_to_all(message, ("core", "phase"), 0, 0, tiled=True)
     devices = ("phase", "ring", "core")
     moves = [(at, at + 1, 0) for at in range(ring - 1)] + [(at + 1, at, 1) for at in range(ring - 1)]
     pairs = [((p * ring + a) * 2 + c, (p * ring + b) * 2 + c) for p in range(TILE) for a, b, c in moves]
-    near = lax.dynamic_slice_in_dim(own, jnp.where(core == 0, 4 * (TILE - 2), 0), 4 * (TILE + 2), 0)
+    near = lax.dynamic_slice_in_dim(own, near_at, 4 * (TILE + 2), 0)
     near = lax.ppermute(near, devices, pairs)
-    far = lax.dynamic_slice_in_dim(near, jnp.where(core == 0, 4 * TILE, 0), 8, 0)
+    far = lax.dynamic_slice_in_dim(near, far_at, 8, 0)
     far = lax.ppermute(far, "core", [(0, 1), (1, 0)])
     columns = tile(lat[None], own, near, far)
     columns = lax.all_to_all(columns, "phase", 0, 0, tiled=True)

time: 51.2 us -> 51.3 us (level)
  blocking collectives: 11.9 us -> 29.8 us
  starting transfers between devices: 15.4 us -> 6.09 us
  waiting for transfers between devices: 11.2 us -> 2.75 us
    all_to_all x0 -> x1, blocking collectives: none -> 17.8 us  [per_device(): own = lax.all_to_all(message, ('core', 'phase'), 0, 0, tiled=True)]
    all_to_all x1 -> x0, starting transfers between devices: 9.29 us -> none  [per_device(): own = lax.all_to_all(message, ('core', 'phase'), 0, 0, tiled=True)]
    all_to_all x1 -> x0, waiting for transfers between devices: 8.51 us -> none  [per_device(): own = lax.all_to_all(message, ('core', 'phase'), 0, 0, tiled=True)]
  transfers between devices with their start and end apart: 3 -> 2, of which waited for: 3 -> 2; matrix products, arithmetic and copies ran while one was open for 0% -> 0% of each run, Pallas kernels for 0% -> 0%
where the time goes in v5:
time: 51.3 us; the launch traced here: 50.9 us
  blocking collectives  29.8 us (58%)
  Pallas kernels  10.3 us (20%)
  starting transfers between devices  6.09 us (12%)
  waiting for transfers between devices  2.75 us (5%)
  between operations  1.96 us (4%)
    all_to_all x1, blocking collectives, per_device(): own = lax.all_to_all(message, ('core', 'phase'), 0, 0, tiled=True)  17.8 us
    all_to_all x1, blocking collectives, per_device(): columns = lax.all_to_all(columns, 'phase', 0, 0, tiled=True)  12 us
    pallas_call x1, Pallas kernels, tile(): pl.pallas_call(tile_kernel, out_shape=jax.ShapeDtypeStruct((TILE, LANES),...  7.28 us
    ppermute x1, starting transfers between devices, per_device(): near = lax.ppermute(near, devices, pairs)  5.49 us
    ppermute x1, waiting for transfers between devices, per_device(): near = lax.ppermute(near, devices, pairs)  1.92 us
    pallas_call x1, Pallas kernels, pack(): pl.pallas_call(pack_kernel, out_shape=jax.ShapeDtypeStruct((2 * TILE * 4,...  1.58 us
    pallas_call x1, Pallas kernels, unpack(): pl.pallas_call(unpack_kernel, out_shape=(shape, shape), in_specs=[vmem(),...  1.41 us
  transfers between devices with their start and end apart: 2, of which 2 were waited for; matrix products, arithmetic and copies ran while one was open for 0% of the time, Pallas kernels for 0%

profile of v5, /device:TPU:64, one launch (start us, length us, event | category | flops | bytes accessed | tf_op | source)
XLA Modules:
  0.0 50.9 jit_solution(6336772366863423439)
XLA Ops:
  1.9 1.6 %pack.1 = f32[256,128]{1,0:T(8,128)} custom-call(s32[1]{0:T(128)} %bitcast.row_ref, f32[1,1]{1,0:T(1,128)} %bitcast.13.time_ref, f32[1,1]{1,0:T(1,128)} %bitcast.14.weight_ref, f32[32]{0:T(128)} %cor_ref.1, f32[3,8,128]{2,1,0:T(8,128)} %bitcast.20, f32[32,1024]{1,0:T(8,128)} %depth_ref.1, f32[24,128]{1,0:T(8,128)} %constant.25.clone.table_ref), custom_call_target="tpu_custom_call" | custom-call | tf_op jit(solution)/shard_map/pack/pallas_call | solution.py:360
  3.5 17.8 %all_to_all.22 = f32[64,4,128]{2,1,0:T(4,128)S(1)} all-to-all(f32[64,4,128]{2,1,0:T(4,128)} %bitcast.18), channel_id=1, replica_groups=mesh['phase'=32,'ring'=4,'core'=2] {'core','phase'}, dimensions={0} | all-to-all | bytes 262144 | tf_op jit(solution)/shard_map/all_to_all | solution.py:413
  21.3 5.5 %collective-permute-start = (f32[136,128]{1,0:T(8,128)S(1)}, f32[136,128]{1,0:T(8,128)S(1)}, u32[]{:S(2)}, u32[]{:S(2)}) collective-permute-start(f32[136,128]{1,0:T(8,128)S(1)} %constant_dynamic-slice_fusion.1), channel_id=1, source_target_pairs={{0,2},{2,4},{4,6},{3,1},{5,3},{7,5},{8,10},{10,12},{12,14},{11,9},... | collective-permute-start | bytes 208904 | tf_op jit(solution)/shard_map/ppermute | solution.py:418
  26.8 1.9 %collective-permute-done.near_ref = f32[136,128]{1,0:T(8,128)S(1)} collective-permute-done((f32[136,128]{1,0:T(8,128)S(1)}, f32[136,128]{1,0:T(8,128)S(1)}, u32[]{:S(2)}, u32[]{:S(2)}) %collective-permute-start) | collective-permute-done | bytes 69664 | tf_op jit(solution)/shard_map/ppermute | solution.py:418
  28.8 0.6 %collective-permute-start.1 = (f32[8,128]{1,0:T(8,128)S(1)}, f32[8,128]{1,0:T(8,128)S(1)}, u32[]{:S(2)}, u32[]{:S(2)}) collective-permute-start(f32[8,128]{1,0:T(8,128)S(1)} %constant_dynamic-slice_fusion), channel_id=1, source_target_pairs={{0,1},{1,0},{2,3},{3,2},{4,5},{5,4},{6,7},{7,6},{8,9},{9,8},{10,11... | collective-permute-start | bytes 12296 | tf_op jit(solution)/shard_map/ppermute | solution.py:420
  29.4 0.8 %collective-permute-done.1.far_ref = f32[8,128]{1,0:T(8,128)S(1)} collective-permute-done((f32[8,128]{1,0:T(8,128)S(1)}, f32[8,128]{1,0:T(8,128)S(1)}, u32[]{:S(2)}, u32[]{:S(2)}) %collective-permute-start.1) | collective-permute-done | bytes 4128 | tf_op jit(solution)/shard_map/ppermute | solution.py:420
  30.2 7.3 %tile.1 = f32[32,128]{1,0:T(8,128)S(1)} custom-call(s32[1]{0:T(128)} %bitcast.4.place_ref, f32[256,128]{1,0:T(8,128)S(1)} %bitcast.16, f32[136,128]{1,0:T(8,128)S(1)} %collective-permute-done.near_ref, f32[8,128]{1,0:T(8,128)S(1)} %collective-permute-done.1.far_ref), custom_call_target="tpu_custom_call" | custom-call | tf_op jit(solution)/shard_map/tile/pallas_call | solution.py:369
  37.5 12.0 %all_to_all.23 = f32[32,1,128]{2,1,0:T(1,128)} all-to-all(f32[32,1,128]{2,1,0:T(1,128)S(1)} %bitcast.17), channel_id=1, replica_groups=mesh['phase'=32,'ring'=4,'core'=2] {'phase'}, dimensions={0} | all-to-all | bytes 32768 | tf_op jit(solution)/shard_map/all_to_all | solution.py:422
  49.5 1.4 %unpack.1 = (f32[3,8,128]{2,1,0:T(8,128)}, f32[3,8,128]{2,1,0:T(8,128)}) custom-call(f32[32,128]{1,0:T(8,128)} %bitcast.19, f32[3,8,128]{2,1,0:T(8,128)} %bitcast.21), custom_call_target="tpu_custom_call" | custom-call | tf_op jit(solution)/shard_map/unpack/pallas_call | solution.py:395
  (2 shorter events, 0.0 us)
Async XLA Ops:
  21.3 7.4 %collective-permute-start = (f32[136,128]{1,0:T(8,128)S(1)}, f32[136,128]{1,0:T(8,128)S(1)}, u32[]{:S(2)}, u32[]{:S(2)}) collective-permute-start(f32[136,128]{1,0:T(8,128)S(1)} %constant_dynamic-slice_fusion.1), channel_id=1, source_target_pairs={{0,2},{2,4},{4,6},{3,1},{5,3},{7,5},{8,10},{10,12},{12,14},{11,9},... | collective-permute-start | bytes 208904 | tf_op jit(solution)/shard_map/ppermute | solution.py:418
  28.8 1.4 %collective-permute-start.1 = (f32[8,128]{1,0:T(8,128)S(1)}, f32[8,128]{1,0:T(8,128)S(1)}, u32[]{:S(2)}, u32[]{:S(2)}) collective-permute-start(f32[8,128]{1,0:T(8,128)S(1)} %constant_dynamic-slice_fusion), channel_id=1, source_target_pairs={{0,1},{1,0},{2,3},{3,2},{4,5},{5,4},{6,7},{7,6},{8,9},{9,8},{10,11... | collective-permute-start | bytes 12296 | tf_op jit(solution)/shard_map/ppermute | solution.py:420

commit v6 on v4

--- a/solution.py
+++ b/solution.py
@@ -106,7 +106,7 @@
 
 def tile_kernel(
     place_ref, own_ref, near_ref, far_ref, out_ref,
-    p_ref, z_ref, w_ref, yh_ref, yl_ref, t_ref, depth_ref, cor_ref, mask_ref, forward_ref, backh_ref, backl_ref,
+    p_ref, z_ref, w_ref, yh_ref, yl_ref, t_ref, depth_ref, cor_ref, mask_ref, forward_ref, back_ref,
 ):
     lat = place_ref[0]
     core = lax.rem(lat, 2)
@@ -173,12 +173,18 @@
     forward = picked(high, pick_high) + picked(low, pick_low)
     forward_ref[...] = jnp.where(same, forward, 0.0).astype(bf16)
     high, low = spread(1)
-    pick = jnp.where((group == term) & (term < TERMS), 1.0, 0.0).astype(bf16)[:, :LANES]
-    back_high = jnp.where(same[:, :LANES], picked(high, pick), 0.0).T
-    back_low = jnp.where(same[:, :LANES], picked(low, pick), 0.0).T
-    backh_ref[0:80, :] = back_high[0:80].astype(bf16)
-    backh_ref[80:160, :] = back_low[0:80].astype(bf16)
-    backl_ref[...] = back_high[0:80].astype(bf16)
+    line = lax.broadcasted_iota(jnp.int32, (80, LANES), 0) // 8
+    term = lax.broadcasted_iota(jnp.int32, (80, LANES), 1)
+    pick = jnp.where((line == term) & (term < TERMS), -0.5, 0.0).astype(bf16)
+
+    def turned(value):
+        value = lax.dot_general(pick, value, (((1,), (1,)), ((), ())), preferred_element_type=f32)
+        return jnp.where(same[:80], value, 0.0).astype(bf16)
+
+    back_high = turned(high)
+    back_ref[:, 0:256] = back_high
+    back_ref[:, 256:512] = turned(low)
+    back_ref[:, 512:768] = back_high
 
     def east(value):
         return pltpu.roll(value, LANES - 1, 1) - pltpu.roll(value, 1, 1)
@@ -253,9 +259,8 @@
             yl_ref[n, pair, :, f * LANES : (f + 1) * LANES] = low
 
     def weighted(n):
-        both = jnp.dot(backh_ref[...], yh_ref[n].reshape(256, WIDE), preferred_element_type=f32)
-        low = jnp.dot(backl_ref[...], yl_ref[n].reshape(256, WIDE), preferred_element_type=f32)
-        return (both[0:80] + both[80:160] + low) * -0.5
+        high, low = yh_ref[n].reshape(256, WIDE), yl_ref[n].reshape(256, WIDE)
+        return jnp.dot(back_ref[...], jnp.concatenate([high, high, low], axis=0), preferred_element_type=f32)
 
     def put(total, row, first, last, turn):
         at = slice(PAD + row + first, PAD + row + last)
@@ -382,8 +387,7 @@
             pltpu.VMEM((ROWS, LANES), f32),
             pltpu.VMEM((ROWS, LANES), f32),
             pltpu.VMEM((256, 256), bf16),
-            pltpu.VMEM((160, 256), bf16),
-            pltpu.VMEM((80, 256), bf16),
+            pltpu.VMEM((80, 768), bf16),
         ],
         compiler_params=pltpu.CompilerParams(vmem_limit_bytes=48 * 1024 * 1024),
         name="tile",

time: 51.2 us -> 51 us (level)
  no operation moved by 1% of the time
where the time goes in v6:
time: 51 us; the launch traced here: 50.6 us
  starting transfers between devices  15.4 us (30%)
  blocking collectives  11.9 us (23%)
  waiting for transfers between devices  11.2 us (22%)
  Pallas kernels  10.1 us (20%)
  between operations  1.97 us (4%)
    all_to_all x1, blocking collectives, per_device(): columns = lax.all_to_all(columns, 'phase', 0, 0, tiled=True)  11.9 us
    all_to_all x1, starting transfers between devices, per_device(): own = lax.all_to_all(message, ('core', 'phase'), 0, 0, tiled=True)  9.29 us
    all_to_all x1, waiting for transfers between devices, per_device(): own = lax.all_to_all(message, ('core', 'phase'), 0, 0, tiled=True)  8.51 us
    pallas_call x1, Pallas kernels, tile(): pl.pallas_call(tile_kernel, out_shape=jax.ShapeDtypeStruct((TILE, LANES),...  7.12 us
    ppermute x1, starting transfers between devices, per_device(): near = lax.ppermute(near, devices, pairs)  5.48 us
    ppermute x1, waiting for transfers between devices, per_device(): near = lax.ppermute(near, devices, pairs)  1.92 us
    pallas_call x1, Pallas kernels, pack(): pl.pallas_call(pack_kernel, out_shape=jax.ShapeDtypeStruct((2 * TILE * 4,...  1.58 us
    pallas_call x1, Pallas kernels, unpack(): pl.pallas_call(unpack_kernel, out_shape=(shape, shape), in_specs=[vmem(),...  1.41 us
  transfers between devices with their start and end apart: 3, of which 3 were waited for; matrix products, arithmetic and copies ran while one was open for 0% of the time, Pallas kernels for 0%

profile of v6, /device:TPU:64, one launch (start us, length us, event | category | flops | bytes accessed | tf_op | source)
XLA Modules:
  0.0 50.6 jit_solution(17540265410552572473)
XLA Ops:
  1.9 1.6 %pack.1 = f32[256,128]{1,0:T(8,128)} custom-call(s32[1]{0:T(128)} %bitcast.1.row_ref, f32[1,1]{1,0:T(1,128)} %bitcast.13.time_ref, f32[1,1]{1,0:T(1,128)} %bitcast.14.weight_ref, f32[32]{0:T(128)} %cor_ref.1, f32[3,8,128]{2,1,0:T(8,128)} %bitcast.20, f32[32,1024]{1,0:T(8,128)} %depth_ref.1, f32[24,128]{1,0:T(8,128)} %constant.27.clone.table_ref), custom_call_target="tpu_custom_call" | custom-call | tf_op jit(solution)/shard_map/pack/pallas_call | solution.py:365
  3.5 9.3 %all-to-all-start = ((f32[64,4,128]{2,1,0:T(4,128)}), f32[64,4,128]{2,1,0:T(4,128)S(1)}, u32[]{:S(2)}, u32[]{:S(2)}) async-start(f32[64,4,128]{2,1,0:T(4,128)} %bitcast.18), calls=%async_computation | async-start | bytes 262144 | tf_op jit(solution)/shard_map/all_to_all | solution.py:414
  12.8 8.5 %all-to-all-done = f32[64,4,128]{2,1,0:T(4,128)S(1)} async-done(((f32[64,4,128]{2,1,0:T(4,128)}), f32[64,4,128]{2,1,0:T(4,128)S(1)}, u32[]{:S(2)}, u32[]{:S(2)}) %all-to-all-start) | async-done | bytes 131104 | tf_op jit(solution)/shard_map/all_to_all | solution.py:414
  21.3 5.5 %collective-permute-start = (f32[136,128]{1,0:T(8,128)S(1)}, f32[136,128]{1,0:T(8,128)S(1)}, u32[]{:S(2)}, u32[]{:S(2)}) collective-permute-start(f32[136,128]{1,0:T(8,128)S(1)} %constant_dynamic-slice_fusion.1), channel_id=1, source_target_pairs={{0,2},{2,4},{4,6},{3,1},{5,3},{7,5},{8,10},{10,12},{12,14},{11,9},... | collective-permute-start | bytes 208904 | tf_op jit(solution)/shard_map/ppermute | solution.py:419
  26.8 1.9 %collective-permute-done.near_ref = f32[136,128]{1,0:T(8,128)S(1)} collective-permute-done((f32[136,128]{1,0:T(8,128)S(1)}, f32[136,128]{1,0:T(8,128)S(1)}, u32[]{:S(2)}, u32[]{:S(2)}) %collective-permute-start) | collective-permute-done | bytes 69664 | tf_op jit(solution)/shard_map/ppermute | solution.py:419
  28.7 0.6 %collective-permute-start.1 = (f32[8,128]{1,0:T(8,128)S(1)}, f32[8,128]{1,0:T(8,128)S(1)}, u32[]{:S(2)}, u32[]{:S(2)}) collective-permute-start(f32[8,128]{1,0:T(8,128)S(1)} %constant_dynamic-slice_fusion), channel_id=1, source_target_pairs={{0,1},{1,0},{2,3},{3,2},{4,5},{5,4},{6,7},{7,6},{8,9},{9,8},{10,11... | collective-permute-start | bytes 12296 | tf_op jit(solution)/shard_map/ppermute | solution.py:421
  29.3 0.8 %collective-permute-done.1.far_ref = f32[8,128]{1,0:T(8,128)S(1)} collective-permute-done((f32[8,128]{1,0:T(8,128)S(1)}, f32[8,128]{1,0:T(8,128)S(1)}, u32[]{:S(2)}, u32[]{:S(2)}) %collective-permute-start.1) | collective-permute-done | bytes 4128 | tf_op jit(solution)/shard_map/ppermute | solution.py:421
  30.2 7.1 %tile.1 = f32[32,128]{1,0:T(8,128)S(1)} custom-call(s32[1]{0:T(128)} %bitcast.place_ref, f32[256,128]{1,0:T(8,128)S(1)} %bitcast.16, f32[136,128]{1,0:T(8,128)S(1)} %collective-permute-done.near_ref, f32[8,128]{1,0:T(8,128)S(1)} %collective-permute-done.1.far_ref), custom_call_target="tpu_custom_call" | custom-call | tf_op jit(solution)/shard_map/tile/pallas_call | solution.py:374
  37.3 11.9 %all_to_all.22 = f32[32,1,128]{2,1,0:T(1,128)} all-to-all(f32[32,1,128]{2,1,0:T(1,128)S(1)} %bitcast.17), channel_id=1, replica_groups=mesh['phase'=32,'ring'=4,'core'=2] {'phase'}, dimensions={0} | all-to-all | bytes 32768 | tf_op jit(solution)/shard_map/all_to_all | solution.py:423
  49.1 1.4 %unpack.1 = (f32[3,8,128]{2,1,0:T(8,128)}, f32[3,8,128]{2,1,0:T(8,128)}) custom-call(f32[32,128]{1,0:T(8,128)} %bitcast.19, f32[3,8,128]{2,1,0:T(8,128)} %bitcast.21), custom_call_target="tpu_custom_call" | custom-call | tf_op jit(solution)/shard_map/unpack/pallas_call | solution.py:399
  (2 shorter events, 0.0 us)
Async XLA Ops:
  3.5 17.8 %all-to-all-start = ((f32[64,4,128]{2,1,0:T(4,128)}), f32[64,4,128]{2,1,0:T(4,128)S(1)}, u32[]{:S(2)}, u32[]{:S(2)}) async-start(f32[64,4,128]{2,1,0:T(4,128)} %bitcast.18), calls=%async_computation | async-start | bytes 262144 | tf_op jit(solution)/shard_map/all_to_all | solution.py:414
  21.3 7.4 %collective-permute-start = (f32[136,128]{1,0:T(8,128)S(1)}, f32[136,128]{1,0:T(8,128)S(1)}, u32[]{:S(2)}, u32[]{:S(2)}) collective-permute-start(f32[136,128]{1,0:T(8,128)S(1)} %constant_dynamic-slice_fusion.1), channel_id=1, source_target_pairs={{0,2},{2,4},{4,6},{3,1},{5,3},{7,5},{8,10},{10,12},{12,14},{11,9},... | collective-permute-start | bytes 208904 | tf_op jit(solution)/shard_map/ppermute | solution.py:419
  28.7 1.4 %collective-permute-start.1 = (f32[8,128]{1,0:T(8,128)S(1)}, f32[8,128]{1,0:T(8,128)S(1)}, u32[]{:S(2)}, u32[]{:S(2)}) collective-permute-start(f32[8,128]{1,0:T(8,128)S(1)} %constant_dynamic-slice_fusion), channel_id=1, source_target_pairs={{0,1},{1,0},{2,3},{3,2},{4,5},{5,4},{6,7},{7,6},{8,9},{9,8},{10,11... | collective-permute-start | bytes 12296 | tf_op jit(solution)/shard_map/ppermute | solution.py:421

commit v7 on v6

--- a/solution.py
+++ b/solution.py
@@ -104,9 +104,44 @@
     return high, (value - high.astype(f32)).astype(bf16)
 
 
+def matrices_kernel(own_ref, forward_ref, back_ref):
+    term = lax.broadcasted_iota(jnp.int32, (LANES, 256), 0)
+    column = lax.broadcasted_iota(jnp.int32, (LANES, 256), 1)
+    group = column // 8
+    high_at = (group == term) | (group - 10 == term)
+    low_at = group - 20 == term
+    pick_high = jnp.where(high_at & (term < TERMS), 1.0, 0.0).astype(bf16)
+    pick_low = jnp.where(low_at & (term < TERMS), 1.0, 0.0).astype(bf16)
+    same = lax.broadcasted_iota(jnp.int32, (256, 256), 0) % 8 == lax.broadcasted_iota(jnp.int32, (256, 256), 1) % 8
+
+    def spread(block):
+        value = own_ref[pl.ds(block, SAMPLES, stride=4), :]
+        return split(jnp.broadcast_to(value[:, None, :], (SAMPLES, 8, LANES)).reshape(256, LANES))
+
+    def picked(value, pick):
+        return jnp.dot(value, pick, preferred_element_type=f32)
+
+    high, low = spread(0)
+    forward = picked(high, pick_high) + picked(low, pick_low)
+    forward_ref[...] = jnp.where(same, forward, 0.0).astype(bf16)
+    high, low = spread(1)
+    line = lax.broadcasted_iota(jnp.int32, (80, LANES), 0) // 8
+    term = lax.broadcasted_iota(jnp.int32, (80, LANES), 1)
+    pick = jnp.where((line == term) & (term < TERMS), -0.5, 0.0).astype(bf16)
+
+    def turned(value):
+        value = lax.dot_general(pick, value, (((1,), (1,)), ((), ())), preferred_element_type=f32)
+        return jnp.where(same[:80], value, 0.0).astype(bf16)
+
+    back_high = turned(high)
+    back_ref[:, 0:256] = back_high
+    back_ref[:, 256:512] = turned(low)
+    back_ref[:, 512:768] = back_high
+
+
 def tile_kernel(
-    place_ref, own_ref, near_ref, far_ref, out_ref,
-    p_ref, z_ref, w_ref, yh_ref, yl_ref, t_ref, depth_ref, cor_ref, mask_ref, forward_ref, back_ref,
+    place_ref, own_ref, near_ref, far_ref, forward_ref, back_ref, out_ref,
+    p_ref, z_ref, w_ref, yh_ref, yl_ref, t_ref, depth_ref, cor_ref, mask_ref,
 ):
     lat = place_ref[0]
     core = lax.rem(lat, 2)
@@ -152,39 +187,6 @@
 
     at_row = lax.broadcasted_iota(jnp.int32, (ROWS, LANES), 0) + (TILE * lat - BASE - PAD)
     mask_ref[...] = jnp.where((at_row >= 0) & (at_row < 8 * TILE), 1.0, 0.0).astype(f32)
-
-    term = lax.broadcasted_iota(jnp.int32, (LANES, 256), 0)
-    column = lax.broadcasted_iota(jnp.int32, (LANES, 256), 1)
-    group = column // 8
-    high_at = (group == term) | (group - 10 == term)
-    low_at = group - 20 == term
-    pick_high = jnp.where(high_at & (term < TERMS), 1.0, 0.0).astype(bf16)
-    pick_low = jnp.where(low_at & (term < TERMS), 1.0, 0.0).astype(bf16)
-    same = lax.broadcasted_iota(jnp.int32, (256, 256), 0) % 8 == lax.broadcasted_iota(jnp.int32, (256, 256), 1) % 8
-
-    def spread(block):
-        value = own_ref[pl.ds(block, SAMPLES, stride=4), :]
-        return split(jnp.broadcast_to(value[:, None, :], (SAMPLES, 8, LANES)).reshape(256, LANES))
-
-    def picked(value, pick):
-        return jnp.dot(value, pick, preferred_element_type=f32)
-
-    high, low = spread(0)
-    forward = picked(high, pick_high) + picked(low, pick_low)
-    forward_ref[...] = jnp.where(same, forward, 0.0).astype(bf16)
-    high, low = spread(1)
-    line = lax.broadcasted_iota(jnp.int32, (80, LANES), 0) // 8
-    term = lax.broadcasted_iota(jnp.int32, (80, LANES), 1)
-    pick = jnp.where((line == term) & (term < TERMS), -0.5, 0.0).astype(bf16)
-
-    def turned(value):
-        value = lax.dot_general(pick, value, (((1,), (1,)), ((), ())), preferred_element_type=f32)
-        return jnp.where(same[:80], value, 0.0).astype(bf16)
-
-    back_high = turned(high)
-    back_ref[:, 0:256] = back_high
-    back_ref[:, 256:512] = turned(low)
-    back_ref[:, 512:768] = back_high
 
     def east(value):
         return pltpu.roll(value, LANES - 1, 1) - pltpu.roll(value, 1, 1)
@@ -370,11 +372,22 @@
     )(row, times.reshape(1, 1), weights.reshape(1, 1), cor, state, depth, jnp.asarray(series_table()))
 
 
-def tile(place, own, near, far):
+def matrices(own):
+    return pl.pallas_call(
+        matrices_kernel,
+        out_shape=(jax.ShapeDtypeStruct((256, 256), bf16), jax.ShapeDtypeStruct((80, 768), bf16)),
+        in_specs=[vmem()],
+        out_specs=(vmem(), vmem()),
+        cost_estimate=pl.CostEstimate(flops=60_000_000, bytes_accessed=400_000, transcendentals=0),
+        name="matrices",
+    )(own)
+
+
+def tile(place, own, near, far, forward, back):
     return pl.pallas_call(
         tile_kernel,
         out_shape=jax.ShapeDtypeStruct((TILE, LANES), f32),
-        in_specs=[smem()] + [vmem()] * 3,
+        in_specs=[smem()] + [vmem()] * 5,
         out_specs=vmem(),
         scratch_shapes=[
             pltpu.VMEM((TERMS + 1, 3, ROWS, LANES), f32),
@@ -386,12 +399,10 @@
             pltpu.VMEM((ROWS, LANES), f32),
             pltpu.VMEM((ROWS, LANES), f32),
             pltpu.VMEM((ROWS, LANES), f32),
-            pltpu.VMEM((256, 256), bf16),
-            pltpu.VMEM((80, 768), bf16),
         ],
         compiler_params=pltpu.CompilerParams(vmem_limit_bytes=48 * 1024 * 1024),
         name="tile",
-    )(place, own, near, far)
+    )(place, own, near, far, forward, back)
 
 
 def unpack(columns, state):
@@ -417,9 +428,10 @@
     pairs = [((p * ring + a) * 2 + c, (p * ring + b) * 2 + c) for p in range(TILE) for a, b, c in moves]
     near = lax.dynamic_slice_in_dim(own, jnp.where(core == 0, 4 * (TILE - 2), 0), 4 * (TILE + 2), 0)
     near = lax.ppermute(near, devices, pairs)
+    near, forward, back = lax.optimization_barrier((near, *matrices(own)))
     far = lax.dynamic_slice_in_dim(near, jnp.where(core == 0, 4 * TILE, 0), 8, 0)
     far = lax.ppermute(far, "core", [(0, 1), (1, 0)])
-    columns = tile(lat[None], own, near, far)
+    columns = tile(lat[None], own, near, far, forward, back)
     columns = lax.all_to_all(columns, "phase", 0, 0, tiled=True)
     state_next, tendency = unpack(columns, state)
     return state_next.reshape(state_now.shape), tendency.reshape(state_now.shape)

time: 51 us -> 54 us (1.059)
  local copies, waits for them, and re-layouts: 0.01 us -> 2.72 us
  Pallas kernels: 10.1 us -> 12 us
  waiting for transfers between devices: 11.2 us -> 9.39 us
    unnamed x0 -> x8, local copies, waits for them, and re-layouts: none -> 2.71 us
    ppermute x1, waiting for transfers between devices: 1.92 us -> 0.06 us  [per_device(): near = lax.ppermute(near, devices, pairs)]
    pallas_call x0 -> x1, Pallas kernels: none -> 1.85 us  [matrices(): pl.pallas_call(matrices_kernel, out_shape=(jax.ShapeDtypeStruct((256, 256...]
  transfers between devices with their start and end apart: 3 -> 3, of which waited for: 3 -> 3; matrix products, arithmetic and copies ran while one was open for 0% -> 0% of each run, Pallas kernels for 0% -> 3%
where the time goes in v7:
time: 54 us; the launch traced here: 53.5 us
  starting transfers between devices  15.4 us (29%)
  Pallas kernels  12 us (22%)
  blocking collectives  12 us (22%)
  waiting for transfers between devices  9.39 us (17%)
  local copies, waits for them, and re-layouts  2.72 us (5%)
  between operations  1.98 us (4%)
    all_to_all x1, blocking collectives, per_device(): columns = lax.all_to_all(columns, 'phase', 0, 0, tiled=True)  12 us
    all_to_all x1, starting transfers between devices, per_device(): own = lax.all_to_all(message, ('core', 'phase'), 0, 0, tiled=True)  9.29 us
    all_to_all x1, waiting for transfers between devices, per_device(): own = lax.all_to_all(message, ('core', 'phase'), 0, 0, tiled=True)  8.51 us
    pallas_call x1, Pallas kernels, tile(): pl.pallas_call(tile_kernel, out_shape=jax.ShapeDtypeStruct((TILE, LANES),...  7.15 us
    ppermute x1, starting transfers between devices, per_device(): near = lax.ppermute(near, devices, pairs)  5.49 us
    unnamed x8, local copies, waits for them, and re-layouts  2.71 us
    pallas_call x1, Pallas kernels, matrices(): pl.pallas_call(matrices_kernel, out_shape=(jax.ShapeDtypeStruct((256, 256...  1.85 us
    pallas_call x1, Pallas kernels, pack(): pl.pallas_call(pack_kernel, out_shape=jax.ShapeDtypeStruct((2 * TILE * 4,...  1.58 us
  transfers between devices with their start and end apart: 3, of which 3 were waited for; matrix products, arithmetic and copies ran while one was open for 0% of the time, Pallas kernels for 3%

profile of v7, /device:TPU:64, one launch (start us, length us, event | category | flops | bytes accessed | tf_op | source)
XLA Modules:
  0.0 53.5 jit_solution(3594248026646248521)
XLA Ops:
  1.9 1.6 %pack.1 = f32[256,128]{1,0:T(8,128)} custom-call(s32[1]{0:T(128)} %bitcast.1.row_ref, f32[1,1]{1,0:T(1,128)} %bitcast.13.time_ref, f32[1,1]{1,0:T(1,128)} %bitcast.14.weight_ref, f32[32]{0:T(128)} %cor_ref.1, f32[3,8,128]{2,1,0:T(8,128)} %bitcast.21, f32[32,1024]{1,0:T(8,128)} %depth_ref.1, f32[24,128]{1,0:T(8,128)} %constant.27.clone.table_ref), custom_call_target="tpu_custom_call" | custom-call | tf_op jit(solution)/shard_map/pack/pallas_call | solution.py:367
  3.5 9.3 %all-to-all-start = ((f32[64,4,128]{2,1,0:T(4,128)}), f32[64,4,128]{2,1,0:T(4,128)S(1)}, u32[]{:S(2)}, u32[]{:S(2)}) async-start(f32[64,4,128]{2,1,0:T(4,128)} %bitcast.19), calls=%async_computation | async-start | bytes 262144 | tf_op jit(solution)/shard_map/all_to_all | solution.py:425
  12.8 8.5 %all-to-all-done = f32[64,4,128]{2,1,0:T(4,128)S(1)} async-done(((f32[64,4,128]{2,1,0:T(4,128)}), f32[64,4,128]{2,1,0:T(4,128)S(1)}, u32[]{:S(2)}, u32[]{:S(2)}) %all-to-all-start) | async-done | bytes 131104 | tf_op jit(solution)/shard_map/all_to_all | solution.py:425
  21.3 0.0 copy-start
  21.3 5.5 %collective-permute-start = (f32[136,128]{1,0:T(8,128)S(1)}, f32[136,128]{1,0:T(8,128)S(1)}, u32[]{:S(2)}, u32[]{:S(2)}) collective-permute-start(f32[136,128]{1,0:T(8,128)S(1)} %constant_dynamic-slice_fusion.1), channel_id=1, source_target_pairs={{0,2},{2,4},{4,6},{3,1},{5,3},{7,5},{8,10},{10,12},{12,14},{11,9},... | collective-permute-start | bytes 208904 | tf_op jit(solution)/shard_map/ppermute | solution.py:430
  26.8 0.0 copy-done
  26.8 1.8 %matrices.1 = (bf16[256,256]{1,0:T(8,128)(2,1)}, bf16[80,768]{1,0:T(8,128)(2,1)}) custom-call(f32[256,128]{1,0:T(8,128)} %bitcast.16), custom_call_target="tpu_custom_call" | custom-call | flops 60000000 | bytes 400000 | tf_op jit(solution)/shard_map/matrices/pallas_call | solution.py:376
  28.7 0.1 collective-permute-done.near_ref
  28.8 0.6 %collective-permute-start.1 = (f32[8,128]{1,0:T(8,128)S(1)}, f32[8,128]{1,0:T(8,128)S(1)}, u32[]{:S(2)}, u32[]{:S(2)}) collective-permute-start(f32[8,128]{1,0:T(8,128)S(1)} %constant_dynamic-slice_fusion), channel_id=1, source_target_pairs={{0,1},{1,0},{2,3},{3,2},{4,5},{5,4},{6,7},{7,6},{8,9},{9,8},{10,11... | collective-permute-start | bytes 12296 | tf_op jit(solution)/shard_map/ppermute | solution.py:433
  29.4 0.8 %collective-permute-done.1.far_ref = f32[8,128]{1,0:T(8,128)S(1)} collective-permute-done((f32[8,128]{1,0:T(8,128)S(1)}, f32[8,128]{1,0:T(8,128)S(1)}, u32[]{:S(2)}, u32[]{:S(2)}) %collective-permute-start.1) | collective-permute-done | bytes 4128 | tf_op jit(solution)/shard_map/ppermute | solution.py:433
  30.2 0.0 copy-start.1
  30.2 0.9 %copy-done.1 = f32[64,4,128]{2,1,0:T(4,128)S(1)} copy-done((f32[64,4,128]{2,1,0:T(4,128)S(1)}, f32[64,4,128]{2,1,0:T(4,128)}, u32[]{:S(2)}) %copy-start.1) | copy-done | bytes 131096
  31.1 0.0 copy-start.2
  31.1 0.9 %copy-done.2 = bf16[256,256]{1,0:T(8,128)(2,1)S(1)} copy-done((bf16[256,256]{1,0:T(8,128)(2,1)S(1)}, bf16[256,256]{1,0:T(8,128)(2,1)}, u32[]{:S(2)}) %copy-start.2) | copy-done | bytes 131096
  32.0 0.0 copy-start.3
  32.0 0.9 %copy-done.3 = bf16[80,768]{1,0:T(8,128)(2,1)S(1)} copy-done((bf16[80,768]{1,0:T(8,128)(2,1)S(1)}, bf16[80,768]{1,0:T(8,128)(2,1)}, u32[]{:S(2)}) %copy-start.3) | copy-done | bytes 122904
  32.9 7.2 %tile.1 = f32[32,128]{1,0:T(8,128)S(1)} custom-call(s32[1]{0:T(128)} %bitcast.place_ref, f32[256,128]{1,0:T(8,128)S(1)} %bitcast.17, f32[136,128]{1,0:T(8,128)S(1)} %collective-permute-done.near_ref, f32[8,128]{1,0:T(8,128)S(1)} %collective-permute-done.1.far_ref, bf16[256,256]{1,0:T(8,128)(2,1)S(1)} %copy-done.2, bf16[80,768]{1,0:T(8,128)(2,1)S(1)} %copy-done.3), custom_call_target="tpu_custom_call" | custom-call | tf_op jit(solution)/shard_map/tile/pallas_call | solution.py:387
  40.1 12.0 %all_to_all.22 = f32[32,1,128]{2,1,0:T(1,128)} all-to-all(f32[32,1,128]{2,1,0:T(1,128)S(1)} %bitcast.18), channel_id=1, replica_groups=mesh['phase'=32,'ring'=4,'core'=2] {'phase'}, dimensions={0} | all-to-all | bytes 32768 | tf_op jit(solution)/shard_map/all_to_all | solution.py:435
  52.1 1.4 %unpack.1 = (f32[3,8,128]{2,1,0:T(8,128)}, f32[3,8,128]{2,1,0:T(8,128)}) custom-call(f32[32,128]{1,0:T(8,128)} %bitcast.20, f32[3,8,128]{2,1,0:T(8,128)} %bitcast.22), custom_call_target="tpu_custom_call" | custom-call | tf_op jit(solution)/shard_map/unpack/pallas_call | solution.py:410
  (2 shorter events, 0.0 us)
Async XLA Ops:
  3.5 17.8 %all-to-all-start = ((f32[64,4,128]{2,1,0:T(4,128)}), f32[64,4,128]{2,1,0:T(4,128)S(1)}, u32[]{:S(2)}, u32[]{:S(2)}) async-start(f32[64,4,128]{2,1,0:T(4,128)} %bitcast.19), calls=%async_computation | async-start | bytes 262144 | tf_op jit(solution)/shard_map/all_to_all | solution.py:425
  21.3 5.5 %copy-start = (f32[64,4,128]{2,1,0:T(4,128)}, f32[64,4,128]{2,1,0:T(4,128)S(1)}, u32[]{:S(2)}) copy-start(f32[64,4,128]{2,1,0:T(4,128)S(1)} %all-to-all-done) | copy-start | bytes 393220
  21.3 7.4 %collective-permute-start = (f32[136,128]{1,0:T(8,128)S(1)}, f32[136,128]{1,0:T(8,128)S(1)}, u32[]{:S(2)}, u32[]{:S(2)}) collective-permute-start(f32[136,128]{1,0:T(8,128)S(1)} %constant_dynamic-slice_fusion.1), channel_id=1, source_target_pairs={{0,2},{2,4},{4,6},{3,1},{5,3},{7,5},{8,10},{10,12},{12,14},{11,9},... | collective-permute-start | bytes 208904 | tf_op jit(solution)/shard_map/ppermute | solution.py:430
  28.8 1.4 %collective-permute-start.1 = (f32[8,128]{1,0:T(8,128)S(1)}, f32[8,128]{1,0:T(8,128)S(1)}, u32[]{:S(2)}, u32[]{:S(2)}) collective-permute-start(f32[8,128]{1,0:T(8,128)S(1)} %constant_dynamic-slice_fusion), channel_id=1, source_target_pairs={{0,1},{1,0},{2,3},{3,2},{4,5},{5,4},{6,7},{7,6},{8,9},{9,8},{10,11... | collective-permute-start | bytes 12296 | tf_op jit(solution)/shard_map/ppermute | solution.py:433
  30.2 0.9 %copy-start.1 = (f32[64,4,128]{2,1,0:T(4,128)S(1)}, f32[64,4,128]{2,1,0:T(4,128)}, u32[]{:S(2)}) copy-start(f32[64,4,128]{2,1,0:T(4,128)} %copy-done) | copy-start | bytes 393220
  31.1 0.9 %copy-start.2 = (bf16[256,256]{1,0:T(8,128)(2,1)S(1)}, bf16[256,256]{1,0:T(8,128)(2,1)}, u32[]{:S(2)}) copy-start(bf16[256,256]{1,0:T(8,128)(2,1)} %get-tuple-element.12.forward_ref) | copy-start | bytes 393220
  32.0 0.9 %copy-start.3 = (bf16[80,768]{1,0:T(8,128)(2,1)S(1)}, bf16[80,768]{1,0:T(8,128)(2,1)}, u32[]{:S(2)}) copy-start(bf16[80,768]{1,0:T(8,128)(2,1)} %get-tuple-element.13.back_ref) | copy-start | bytes 368644
